TPU v7x, 512 devices: a whole 4x8x8 slice. The times are simulated.
512 devices in a mesh: views: 8 (over x, z_hi), depth: 64 (over y, z_lo, core).
Axes of the slice: x: 4, y: 8, z: 8 (z_hi: 2, z_lo: 4; z = z_hi * 4 + z_lo), core: 2. Of those that a mesh axis runs over, the one named last changes fastest.
Arguments:
- concentration: float32 [8, 1, 2048, 1024], P(None, None, 'depth'), may hold values from 0 to 1
- shear_index: int32 [16, 2048, 1024], P('views', 'depth'), may hold values from 0 to 1022, as said below
- shear_weight: float32 [16, 2048, 1024], P('views', 'depth'), may hold values from 0 to 1
- attenuation: float32 [4, 8], replicated, may hold values from 2.4414063e-05 to 0.00048828125
- yields: float32 [8], replicated, may hold values from 0.5 to 2
- line_energy: int32 [8], replicated, may hold values from 0 to 2
- measured: float32 [16, 8, 1, 1024], P('views'), may hold values from -4 to 4
Outputs:
- gradient: float32 [8, 1, 2048, 1024], P(None, None, 'depth')
- signal: float32 [16, 8, 1, 1024], P('views')
Inputs may be any that keep to these rules, and one draw needn't show every extreme that they name: shear_index[v, d, t] is t plus a shift of that view and depth cell, the shift between -128 and 128, clipped to the grid.
All inputs are finite; a program needn't handle non-finite values.
Results may differ from a plain program's by a relative error of at most 0.0001.
Values sent between devices are 32-bit elements; how exact they have to be, the bound alone decides.
A program may use at most 64 MiB of HBM per device.

v0:
```python
import jax
import jax.numpy as jnp
from jax import lax
from jax.sharding import PartitionSpec as P


def carried_in(value, axis, combine, identity, reverse):
    size, here = (lax.axis_size(axis), lax.axis_index(axis))
    everything = lax.all_gather(value, axis)
    start = jnp.broadcast_to(jnp.asarray(identity, value.dtype), value.shape)

    def turn(k, before):
        at = size - 1 - k if reverse else k
        reached = at > here if reverse else at < here
        new = combine(before, everything[at])
        return jnp.where(reached, new, before)

    return lax.fori_loop(0, size, turn, start)


def added(first, second):
    return first + second


def fold_edges(padded, margin, width):
    core = padded[..., margin : width - 1 + margin]
    low = jnp.sum(padded[..., :margin], axis=-1)
    high = jnp.sum(padded[..., width - 1 + margin :], axis=-1)
    core = core.at[..., 0].add(low)
    return core.at[..., width - 2].add(high)


def body(concentration, shear_index, shear_weight, attenuation, yields, line_energy, measured):
    elements, rows, slab, width = concentration.shape
    emissions = attenuation.shape[0] - 1
    depth_total = slab * lax.axis_size("depth")
    highest = lax.Precision.HIGHEST
    margin = width // 8
    selector = (line_energy[:, None] == jnp.arange(emissions, dtype=jnp.int32)[None, :]).astype(
        jnp.float32
    )
    starts = shear_index[:, :, width // 2] - width // 2 + margin
    weight_full = shear_weight[:, None, None]
    pairs = jnp.stack([concentration[..., : width - 1], concentration[..., 1:]])
    sources = jnp.pad(pairs, ((0, 0), (0, 0), (0, 0), (0, 0), (margin, margin + 1)), mode="edge")

    def take_row(source_row, offset):
        return lax.dynamic_slice_in_dim(source_row, offset, width, axis=-1)

    by_depth = jax.vmap(take_row, in_axes=(3, 0), out_axes=3)
    by_view = jax.vmap(by_depth, in_axes=(None, 0), out_axes=1)
    sliced = by_view(sources, starts)
    field = sliced[0] * (1.0 - weight_full) + sliced[1] * weight_full
    absorb = jnp.einsum("ke,verdw->vkrdw", attenuation, field, precision=highest)
    running = jnp.cumsum(absorb, axis=3)
    slab_sum = running[:, :, :, -1]
    before = carried_in(slab_sum[:, 0], "depth", added, jnp.zeros_like(slab_sum[:, 0]), False)
    after = carried_in(slab_sum[:, 1:], "depth", added, jnp.zeros_like(slab_sum[:, 1:]), True)
    incident_depth = before[:, :, None] + running[:, 0] - absorb[:, 0]
    exit_depth = after[:, :, :, None] + slab_sum[:, 1:, :, None] - running[:, 1:]
    incident = jnp.exp(-incident_depth)
    leaving = jnp.exp(-exit_depth)
    leaving_line = jnp.einsum("lk,vkrdw->vlrdw", selector, leaving, precision=highest)
    emitted = (
        yields[None, :, None, None, None] * field * incident[:, None] * leaving_line / depth_total
    )
    signal = lax.psum(jnp.sum(emitted, axis=3), "depth")
    misfit = signal - measured
    weighted = misfit[:, :, :, None, :] * emitted
    backward = jnp.sum(weighted, axis=1)
    back_run = jnp.cumsum(backward, axis=2)
    forward = jnp.einsum("lk,vlrdw->vkrdw", selector, weighted, precision=highest)
    fore_run = jnp.cumsum(forward, axis=3)
    later = carried_in(back_run[:, :, -1], "depth", added, jnp.zeros_like(back_run[:, :, -1]), True)
    earlier = carried_in(
        fore_run[:, :, :, -1], "depth", added, jnp.zeros_like(fore_run[:, :, :, -1]), False
    )
    suffix = later[:, :, None] + back_run[:, :, -1:] - back_run
    prefix = earlier[:, :, :, None] + fore_run - forward
    direct = (
        misfit[:, :, :, None, :]
        * yields[None, :, None, None, None]
        * incident[:, None]
        * leaving_line
    )
    view_grad = direct - depth_total * (
        attenuation[0][None, :, None, None, None] * suffix[:, None]
        + jnp.einsum("ke,vkrdw->verdw", attenuation[1:], prefix, precision=highest)
    )
    shares = jnp.stack([view_grad * (1.0 - weight_full), view_grad * weight_full])
    shares_padded = jnp.pad(
        shares, ((0, 0), (0, 0), (0, 0), (0, 0), (0, 0), (2 * margin, 2 * margin))
    )

    def shift_row(values_row, offset):
        return lax.dynamic_slice_in_dim(
            values_row, 2 * margin - offset, width + 2 * margin, axis=-1
        )

    shift_depth = jax.vmap(shift_row, in_axes=(3, 0), out_axes=3)
    shift_view = jax.vmap(shift_depth, in_axes=(1, 0), out_axes=1)
    placed = jnp.sum(shift_view(shares_padded, starts), axis=1)
    folded = fold_edges(placed, margin, width)
    edge_pad_low = ((0, 0), (0, 0), (0, 0), (0, 1))
    edge_pad_high = ((0, 0), (0, 0), (0, 0), (1, 0))
    local = jnp.pad(folded[0], edge_pad_low) + jnp.pad(folded[1], edge_pad_high)
    gradient = lax.psum(local, "views")
    return (gradient, signal)


def solution(mesh):
    return jax.shard_map(
        body,
        mesh=mesh,
        in_specs=(
            P(None, None, "depth", None),
            P("views", "depth", None),
            P("views", "depth", None),
            P(),
            P(),
            P(),
            P("views", None, None, None),
        ),
        out_specs=(P(None, None, "depth", None), P("views", None, None, None)),
        check_vma=False,
    )
```

profile of v0, /device:TPU:1, one launch (start us, length us, event | category | flops | bytes accessed | tf_op | source)
XLA Modules:
  0.0 1612.1 jit_solution(4448392334098317435)
XLA Ops:
  13.5 242.6 %while.64 = (s32[]{:T(128)}, f32[32,2,8,1,1280]{4,0,3,2,1:T(8,128)}, s32[64,5]{0,1:T(8,128)S(1)}, f32[64,2,8,1,1024]{4,2,0,1,3:T(8,128)}, s32[]{:T(128)}) while((s32[]{:T(128)}, f32[32,2,8,1,1280]{4,0,3,2,1:T(8,128)}, s32[64,5]{0,1:T(8,128)S(1)}, f32[64,2,8,1,1024]{4,2,0,1,3:T(8,128)}, s32[]{:T(128)}) %tuple.218), condition=%wide.while_cond.2, body=%wide.while_body.2.sunk | while | flops 2 | bytes 262785 | solution.py:48
  256.1 4.6 fusion.7
  264.5 85.3 %all-gather = f32[128,1,1,1024]{3,2,1,0:T(1,128)S(1)} all-gather(f32[2,1,1,1024]{3,2,1,0:T(1,128)S(1)} %slice.221), channel_id=2, replica_groups=mesh['views'=8,'depth'=64] {'depth'}, dimensions={0}, use_global_device_ids=true | all-gather | bytes 532480 | tf_op jit(solution)/shard_map/all_gather | solution.py:9
  349.9 3.0 while.66
  353.7 34.9 %all-gather.7.cloned.1.call-done = f32[128,3,1,1024]{3,2,1,0:T(1,128)} async-done(((f32[2,3,1,1024]{3,2,1,0:T(1,128)}), f32[128,3,1,1024]{3,2,1,0:T(1,128)}) %all-gather.7.cloned.1.call-update) | async-done | bytes 1572880 | tf_op jit(solution)/shard_map/all_gather | solution.py:9
  388.7 51.8 %while.67 = (s32[]{:T(128)}, f32[2,3,1,1024]{3,2,1,0:T(1,128)S(1)}, s32[]{:T(128)}, f32[64,2,3,1,1024]{4,3,2,1,0:T(1,128)}, s32[]{:T(128)}, /*index=5*/s32[]{:T(128)}, s32[]{:T(128)}, s32[]{:T(128)}) while((s32[]{:T(128)}, f32[2,3,1,1024]{3,2,1,0:T(1,128)S(1)}, s32[]{:T(128)}, f32[64,2,3,1,1024]{4,3,2,1,0:T(1,128)}, s32[]{:T(128)}, ...), condition=%wide.region_4.5_spmd.clone, body=%wide.region_3.4_spmd.clone.sunk | while | flops 18440 | bytes 73883 | solution.py:18
  440.8 5.1 multiply_reduce_fusion
  446.7 459.9 %all-reduce.6.cloned.1.call-done = f32[2,8,1,1024]{3,2,1,0:T(1,128)} async-done(((f32[2,8,1,1024]{3,2,1,0:T(1,128)}), f32[2,8,1,1024]{3,2,1,0:T(1,128)}) %all-reduce.6.cloned.1.call-update) | async-done | bytes 65552 | tf_op jit(solution)/shard_map/psum | solution.py:67
  912.1 85.0 %all-gather.2 = f32[128,1,1,1024]{3,2,1,0:T(1,128)} all-gather(f32[2,1,1,1024]{3,2,1,0:T(1,128)S(1)} %slice.226), channel_id=4, replica_groups=mesh['views'=8,'depth'=64] {'depth'}, dimensions={0}, use_global_device_ids=true | all-gather | bytes 532480 | tf_op jit(solution)/shard_map/all_gather | solution.py:9
  1002.8 47.8 %while.68 = (s32[]{:T(128)}, f32[2,1,1024]{2,1,0:T(1,128)S(1)}, s32[]{:T(128)}, f32[64,2,1,1024]{3,2,1,0:T(1,128)}, s32[]{:T(128)}, /*index=5*/s32[]{:T(128)}, s32[]{:T(128)}, s32[]{:T(128)}) while((s32[]{:T(128)}, f32[2,1,1024]{2,1,0:T(1,128)S(1)}, s32[]{:T(128)}, f32[64,2,1,1024]{3,2,1,0:T(1,128)}, s32[]{:T(128)}, ...), condition=%wide.region_10.11_spmd.clone, body=%wide.region_9.10_spmd.clone.sunk | while | flops 6152 | bytes 24731 | solution.py:18
  1053.1 65.7 %all-gather.9.cloned.1.call-done = f32[128,3,1,1,1024]{4,3,2,1,0:T(1,128)} async-done(((f32[2,3,1,1,1024]{4,3,2,1,0:T(1,128)}), f32[128,3,1,1,1024]{4,3,2,1,0:T(1,128)}) %all-gather.9.cloned.1.call-update) | async-done | bytes 1572880 | tf_op jit(solution)/shard_map/all_gather | solution.py:9
  1118.8 51.4 %while.69 = (s32[]{:T(128)}, f32[2,3,1,1024]{3,2,1,0:T(1,128)S(1)}, s32[]{:T(128)}, f32[64,2,3,1,1024]{4,3,2,1,0:T(1,128)}, s32[]{:T(128)}, /*index=5*/s32[]{:T(128)}) while((s32[]{:T(128)}, f32[2,3,1,1024]{3,2,1,0:T(1,128)S(1)}, s32[]{:T(128)}, f32[64,2,3,1,1024]{4,3,2,1,0:T(1,128)}, s32[]{:T(128)}, ...), condition=%wide.region_13.14_spmd.clone, body=%wide.region_12.13_spmd.clone.sunk | while | flops 18436 | bytes 73821 | solution.py:18
  1170.3 4.8 multiply_bitcast_fusion.1
  1175.1 3.4 fusion
  1178.5 274.4 %while.65 = (s32[]{:T(128)}, f32[2,32,2,8,1,1536]{5,3,1,0,4,2:T(8,128)}, s32[64,6]{0,1:T(8,128)S(1)}, f32[64,2,8,1,1280]{4,2,3,1,0:T(8,128)}, s32[]{:T(128)}) while((s32[]{:T(128)}, f32[2,32,2,8,1,1536]{5,3,1,0,4,2:T(8,128)}, s32[64,6]{0,1:T(8,128)S(1)}, f32[64,2,8,1,1280]{4,2,3,1,0:T(8,128)}, s32[]{:T(128)}) %tuple.206), condition=%wide.while_cond.3, body=%wide.while_body.3.sunk | while | flops 2 | bytes 492181 | solution.py:96
  1196.3 2.9 constant_dynamic-slice_fusion.8
  1204.9 2.9 constant_dynamic-slice_fusion.8
  1217.7 2.9 constant_dynamic-slice_fusion.8
  1226.3 2.9 constant_dynamic-slice_fusion.8
  1239.2 2.9 constant_dynamic-slice_fusion.8
  1247.8 2.9 constant_dynamic-slice_fusion.8
  1252.0 2.9 constant_dynamic-slice_fusion.8
  1256.3 2.9 constant_dynamic-slice_fusion.8
  1269.2 2.9 constant_dynamic-slice_fusion.8
  1273.5 2.9 constant_dynamic-slice_fusion.8
  1277.8 2.9 constant_dynamic-slice_fusion.8
  1282.1 2.9 constant_dynamic-slice_fusion.8
  1290.6 2.9 constant_dynamic-slice_fusion.8
  1299.2 2.9 constant_dynamic-slice_fusion.8
  1452.9 3.1 reduce.10
  1461.9 6.3 scatter-add.9
  1471.2 131.0 %all-reduce.8.cloned.1.call-done = f32[8,1,32,1024]{3,0,2,1:T(8,128)} async-done(((f32[8,1,32,1024]{3,0,2,1:T(8,128)}), f32[8,1,32,1024]{3,0,2,1:T(8,128)}) %all-reduce.8.cloned.1.call-update) | async-done | bytes 1048592 | tf_op jit(solution)/shard_map/psum | solution.py:107
  (914 shorter events, 660.4 us)
Async XLA Ops:
  7.2 381.5 %all-gather.7.cloned.1.call-start = ((), (), s32[]{:S(2)}) async-start(), calls=%async_computation.2 | async-start | bytes 1597440 | tf_op jit(solution)/shard_map/all_gather | solution.py:9
  11.1 245.0 %copy-start.1 = (f32[2,32,1024]{2,1,0:T(8,128)S(1)}, f32[2,32,1024]{2,1,0:T(8,128)}, u32[]{:S(2)}) copy-start(f32[2,32,1024]{2,1,0:T(8,128)} %param.21) | copy-start | bytes 786436
  11.1 245.0 %copy-start.7 = (f32[4,8]{1,0:T(4,128)S(1)}, f32[4,8]{1,0:T(4,128)}, u32[]{:S(2)}) copy-start(f32[4,8]{1,0:T(4,128)} %param.22) | copy-start | bytes 388
  256.1 5.2 copy-start.2
  263.8 177.0 %copy-start.8 = (f32[8]{0:T(128)S(1)}, f32[8]{0:T(128)}, u32[]{:S(2)}) copy-start(f32[8]{0:T(128)} %param.23) | copy-start | bytes 100
  263.8 177.0 %copy-start.9 = (s32[8]{0:T(128)S(1)}, s32[8]{0:T(128)}, u32[]{:S(2)}) copy-start(s32[8]{0:T(128)} %param.24) | copy-start | bytes 100
  264.4 642.2 %all-reduce.6.cloned.1.call-start = ((), (), s32[]{:S(2)}) async-start(), calls=%async_computation | async-start | bytes 131072 | tf_op jit(solution)/shard_map/psum | solution.py:67
  353.7 87.0 %copy-start.3 = (f32[2,32,1024]{2,1,0:T(8,128)S(1)}, f32[2,32,1024]{2,1,0:T(8,128)}, u32[]{:S(2)}) copy-start(f32[2,32,1024]{2,1,0:T(8,128)} %fusion.34) | copy-start | bytes 786436
  440.8 465.8 %copy-start.6 = (f32[2,8,1,1024]{3,2,1,0:T(1,128)S(1)}, f32[2,8,1,1024]{3,2,1,0:T(1,128)}, u32[]{:S(2)}) copy-start(f32[2,8,1,1024]{3,2,1,0:T(1,128)} %param.25) | copy-start | bytes 196612
  446.6 672.3 %all-gather.9.cloned.1.call-start = ((), (), s32[]{:S(2)}) async-start(), calls=%async_computation.3 | async-start | bytes 1597440 | tf_op jit(solution)/shard_map/all_gather | solution.py:9
  911.4 0.7 copy-start.4
  997.1 173.2 %copy-start = (f32[2,32,1024,8]{2,3,1,0:T(8,128)S(1)}, f32[2,32,1024,8]{2,3,1,0:T(8,128)}, u32[]{:S(2)}) copy-start(f32[2,32,1024,8]{2,3,1,0:T(8,128)} %get-tuple-element.595) | copy-start | bytes 6291460
  1002.7 599.4 %all-reduce.8.cloned.1.call-start = ((), (), s32[]{:S(2)}) async-start(), calls=%async_computation.1 | async-start | bytes 2097152 | tf_op jit(solution)/shard_map/psum | solution.py:107
  1471.2 133.8 %copy-start.5 = (f32[2,8,1,1024]{3,2,1,0:T(1,128)S(1)}, f32[2,8,1,1024]{3,2,1,0:T(1,128)}, u32[]{:S(2)}) copy-start(f32[2,8,1,1024]{3,2,1,0:T(1,128)} %all-reduce.6.cloned.1.call-done) | copy-start | bytes 196612
Sparse Core Ops, SparseCore 0:
  264.6 124.0 all-gather.6
  446.7 459.8 all-reduce.5
  1002.8 115.9 all-gather.8
  1471.3 130.7 all-reduce.7
where the time goes:
time: 1630 us; the launch traced here: 1610 us
  waiting for transfers between devices  692 us (42%)
  local copies, waits for them, and re-layouts  542 us (33%)
  other arithmetic  170 us (10%)
  blocking collectives  170 us (10%)
    gather x576, local copies, waits for them, and re-layouts  516 us
    psum x1, waiting for transfers between devices, body(): signal = lax.psum(jnp.sum(emitted, axis=3), 'depth')  460 us
    all_gather x2, blocking collectives, carried_in(): everything = lax.all_gather(value, axis)  170 us
    select_n x256, other arithmetic, turn(): return jnp.where(reached, new, before)  148 us
    psum x1, waiting for transfers between devices, body(): gradient = lax.psum(local, 'views')  131 us
    all_gather x2, waiting for transfers between devices, carried_in(): everything = lax.all_gather(value, axis)  101 us
  transfers between devices with their start and end apart: 4, of which 4 were waited for; matrix products, arithmetic and copies ran while one was open for 3% of the time, Pallas kernels for 0%

commit v1 on v0

v1 whole, which is shorter than its diff:
```python
import functools

import jax
import jax.numpy as jnp
from jax import lax
from jax.experimental import pallas as pl
from jax.experimental.pallas import tpu as pltpu
from jax.sharding import PartitionSpec as P

LANES = 128
TILE = 8
STEP = 256
MESH = pl.DeviceIdType.MESH
F32 = jnp.float32
BF16 = jnp.bfloat16


def split(value):
    high = value.astype(BF16)
    low = (value - high.astype(F32)).astype(BF16)
    return high, low


def dot3(high_ref, low_ref, right):
    right_high, right_low = split(right)
    high = high_ref[...]
    result = jnp.dot(high, right_high, preferred_element_type=F32)
    result += jnp.dot(high, right_low, preferred_element_type=F32)
    return result + jnp.dot(low_ref[...], right_high, preferred_element_type=F32)


def kernel(
    sizes,
    starts,
    att,
    yields,
    line,
    conc,
    weight,
    measured,
    grad,
    signal,
    mat_high,
    mat_low,
    adj_high,
    adj_low,
    pad_left,
    pad_step,
    field,
    decay,
    spread_left,
    spread_right,
    corr,
    slab,
    group,
    local_scale,
    local_part,
    group_send,
    group_recv,
    group_scale,
    back,
    seeds,
    total_send,
    part,
    from_x,
    z_out,
    from_z,
    send1,
    recv1,
    send2,
    recv2,
    send3,
    recv3,
    send4,
    recv4,
    send5,
    recv5,
    send6,
    recv6,
    send7,
    recv7,
    send8,
):
    nx, nz, ny, nc = sizes
    views, depth, width = weight.shape
    blocks = width // LANES
    wide = views * width // nc
    per_view = width // wide
    depth_total = depth * ny * nc
    vi, di = lax.axis_index("views"), lax.axis_index("depth")
    x, zh = vi // nz, vi % nz
    y, c = di // nc, di % nc

    def in_group(k):
        return y * nc + k

    def in_y(k):
        return k * nc + c

    def in_x(k):
        return k * nz + zh

    def in_z(k):
        return x * nz + k

    barrier = pltpu.get_barrier_semaphore()
    greeted = 0
    for k in range(1, nc):
        pl.semaphore_signal(barrier, inc=1, device_id={"depth": in_group((c + k) % nc)}, device_id_type=MESH)
        greeted += 1
    for k in range(1, ny):
        pl.semaphore_signal(barrier, inc=1, device_id={"depth": in_y((y + k) % ny)}, device_id_type=MESH)
        greeted += 1
    for k in range(1, nx):
        pl.semaphore_signal(barrier, inc=1, device_id={"views": in_x((x + k) % nx)}, device_id_type=MESH)
        greeted += 1
    for k in range(1, nz):
        pl.semaphore_signal(barrier, inc=1, device_id={"views": in_z((zh + k) % nz)}, device_id_type=MESH)
        greeted += 1

    rows16 = lax.broadcasted_iota(jnp.int32, (2 * TILE, depth * TILE), 0)
    cols16 = lax.broadcasted_iota(jnp.int32, (2 * TILE, depth * TILE), 1)
    row_item, col_item, col_depth = rows16 & (TILE - 1), cols16 & (TILE - 1), cols16 // TILE

    def spread(item, values):
        result = jnp.full(item.shape, values[0])
        for i in range(1, TILE):
            result = jnp.where(item == i, values[i], result)
        return result

    att_col = [spread(col_item, [att[k, e] for e in range(TILE)]) for k in range(4)]
    att_row = [spread(row_item, [att[k, e] for e in range(TILE)]) for k in range(4)]
    line_col = spread(col_item, [line[e] for e in range(TILE)])
    line_row = spread(row_item, [line[e] for e in range(TILE)])

    def pick(which, options):
        return jnp.where(which == 0, options[0], jnp.where(which == 1, options[1], options[2]))

    forward_out = pick(line_row, att_col[1:])
    adjoint_out = pick(line_col, att_row[1:])
    for i in range(depth // 2):
        here = rows16 // TILE + 2 * i
        rows = pl.ds(2 * TILE * i, 2 * TILE)
        mat = jnp.where(col_depth < here, att_col[0], jnp.where(col_depth > here, forward_out, 0.0))
        mat_high[rows, :], mat_low[rows, :] = split(mat)
        adj = jnp.where(col_depth > here, att_row[0], jnp.where(col_depth < here, adjoint_out, 0.0))
        adj_high[rows, :], adj_low[rows, :] = split(adj)
    att_tile = [value[:TILE, :LANES] for value in att_row]
    line_tile = line_row[:TILE, :LANES]
    yield_tile = spread(row_item[:TILE, :LANES], [yields[e] for e in range(TILE)])

    def over(tile, columns):
        return jnp.concatenate([tile] * (columns // LANES), axis=1)

    lane = lax.broadcasted_iota(jnp.int32, (TILE, LANES), 1)
    sub = lax.broadcasted_iota(jnp.int32, (TILE, LANES), 0)

    def turn_rows(i, carry):
        at = pl.ds(pl.multiple_of(i * TILE, TILE), TILE)
        for j in range(blocks):
            columns = slice(j * LANES, (j + 1) * LANES)
            part[at, :, columns] = jnp.transpose(conc[:, at, columns], (1, 0, 2))
        return carry

    lax.fori_loop(0, depth // TILE, turn_rows, 0)

    def pad_row(d, carry):
        x_blocks = [part[d, :, j * LANES : (j + 1) * LANES] for j in range(blocks)]
        turned = [pltpu.roll(block, LANES - 1, 1) for block in x_blocks]

        def lane_of(block, at):
            return jnp.broadcast_to(block[:, at : at + 1], (TILE, LANES))

        first, second = lane_of(x_blocks[0], 0), lane_of(x_blocks[0], 1)
        before_last, last = lane_of(x_blocks[-1], LANES - 2), lane_of(x_blocks[-1], LANES - 1)
        pad_left[d, 0] = first
        pad_step[d, 0] = second - first
        for j in range(blocks):
            if j < blocks - 1:
                left = x_blocks[j]
                right = jnp.where(lane == LANES - 1, turned[j + 1], turned[j])
            else:
                left = jnp.where(lane == LANES - 1, before_last, x_blocks[j])
                right = jnp.where(lane == LANES - 1, last, turned[j])
            pad_left[d, j + 1] = left
            pad_step[d, j + 1] = right - left
        for j in (blocks + 1, blocks + 2):
            pad_left[d, j] = before_last
            pad_step[d, j] = last - before_last
        return carry

    lax.fori_loop(0, depth, pad_row, 0, unroll=2)

    for v in range(views):

        def take_row(d, row, shares, sums):
            start = starts[v, d]
            block, rest = start >> 7, start & (LANES - 1)
            turn = (LANES - rest) & (LANES - 1)
            left = pltpu.roll(pad_left[d, pl.ds(block, blocks + 1)], turn, 2)
            step = pltpu.roll(pad_step[d, pl.ds(block, blocks + 1)], turn, 2)
            whole = lane < LANES - rest
            new = []
            for j in range(blocks):
                at = pl.ds(j * LANES, LANES)
                share = jnp.broadcast_to(shares[row : row + 1, j * LANES : (j + 1) * LANES], (TILE, LANES))
                value = jnp.where(whole, left[j], left[j + 1]) + share * jnp.where(whole, step[j], step[j + 1])
                field[v, pl.ds(pl.multiple_of(d * TILE, TILE), TILE), at] = value
                new.append(sums[j] + value)
            return tuple(new)

        def take_rows(i, sums):
            base = pl.multiple_of(i * TILE, TILE)
            shares = weight[v, pl.ds(base, TILE), :]
            for row in range(TILE):
                sums = take_row(base + row, row, shares, sums)
            return sums

        zero = jnp.zeros((TILE, LANES), F32)
        sums = lax.fori_loop(0, depth // TILE, take_rows, (zero,) * blocks)
        for j in range(blocks):
            chunk, offset = divmod((v * width + j * LANES), wide)
            absorbed = jnp.zeros((TILE, LANES), F32)
            for k in range(4):
                level = jnp.sum(att_tile[k] * sums[j], axis=0, keepdims=True)
                absorbed = jnp.where(sub == k, jnp.broadcast_to(level, (TILE, LANES)), absorbed)
            slab[chunk, TILE:, offset : offset + LANES] = absorbed

    pl.semaphore_wait(barrier, greeted)

    def to_group(k):
        return pltpu.make_async_remote_copy(
            src_ref=slab.at[k],
            dst_ref=group.at[c],
            send_sem=send1.at[k],
            recv_sem=recv1.at[c],
            device_id={"depth": in_group(k)},
            device_id_type=MESH,
        )

    def emit(i, carry):
        chunk = (c + 1 + i) % nc
        v, base = chunk // per_view, (chunk % per_view) * wide
        for part_at in range(0, wide, STEP):
            at = pl.ds(pl.multiple_of(base + part_at, STEP), STEP)
            values = field[v, :, at]
            value = jnp.exp(-dot3(mat_high, mat_low, values))
            decay[v, :, at] = value
            value = (value * values).reshape(depth, TILE, STEP)
            slab[chunk, :TILE, part_at : part_at + STEP] = jnp.sum(value, axis=0) * over(yield_tile, STEP)

        @pl.when(chunk != c)
        def _():
            to_group(chunk).start()

        return carry

    lax.fori_loop(0, nc, emit, 0)
    group[c] = slab[c]

    def from_group(k):
        return pltpu.make_async_remote_copy(
            src_ref=slab.at[k],
            dst_ref=group.at[k],
            send_sem=send1.at[k],
            recv_sem=recv1.at[k],
            device_id={"depth": in_group(k)},
            device_id_type=MESH,
        )

    for k in range(1, nc):
        from_group((c + k) % nc).wait_recv()

    line_wide = over(line_tile, wide)
    att_wide = [over(tile, wide) for tile in att_tile]

    def scales(ref, count):
        first, later = [], []
        for j in range(count):
            levels = [jnp.broadcast_to(ref[j, TILE + k : TILE + k + 1, :], (TILE, wide)) for k in range(4)]
            first.append(levels[0])
            later.append(pick(line_wide, levels[1:]))
        after = [None] * count
        run = jnp.zeros((TILE, wide), F32)
        for j in reversed(range(count)):
            after[j] = run
            run = run + later[j]
        result = []
        run = jnp.zeros((TILE, wide), F32)
        for j in range(count):
            result.append(jnp.exp(-(run + after[j])))
            run = run + first[j]
        return result

    emitted_sum = jnp.zeros((TILE, wide), F32)
    absorbed_sum = jnp.zeros((TILE, wide), F32)
    for j, scale in enumerate(scales(group, nc)):
        piece = group[j, :TILE, :] * scale
        local_scale[j] = scale
        local_part[j] = piece
        emitted_sum += piece
        absorbed_sum += group[j, TILE:, :]
    group_send[:TILE, :] = emitted_sum
    group_send[TILE:, :] = absorbed_sum

    def y_copy(peer, slot):
        return pltpu.make_async_remote_copy(
            src_ref=group_send,
            dst_ref=group_recv.at[slot],
            send_sem=send2.at[peer],
            recv_sem=recv2.at[slot],
            device_id={"depth": in_y(peer)},
            device_id_type=MESH,
        )

    for k in range(1, ny):
        y_copy((y + k) % ny, y).start()
    group_recv[y] = group_send[...]
    for k in range(1, ny):
        y_copy((y + k) % ny, (y + k) % ny).wait_recv()

    total = jnp.zeros((TILE, wide), F32)
    prior = jnp.zeros((TILE, wide), F32)
    following = jnp.zeros((TILE, wide), F32)
    for j, scale in enumerate(scales(group_recv, ny)):
        piece = group_recv[j, :TILE, :] * scale
        group_scale[j] = scale
        total += piece
        prior += jnp.where(j < y, piece, 0.0)
        following += jnp.where(j > y, piece, 0.0)
    own_view, own_base = c // per_view, pl.multiple_of((c % per_view) * wide, LANES)
    own_at = pl.ds(own_base, wide)
    counts = total * (1.0 / depth_total)
    misfit = counts - measured[own_view, :, own_at]
    here_scale = group_scale[y]
    run = following
    for j in reversed(range(nc)):
        level = jnp.sum(misfit * run, axis=0, keepdims=True)
        back[j, TILE:, :] = att_wide[0] * level
        run = run + local_part[j] * here_scale
    run = prior
    yield_wide = over(yield_tile, wide)
    for j in range(nc):
        back[j, :TILE, :] = misfit * yield_wide * local_scale[j] * here_scale
        mixed = misfit * run
        extra = jnp.zeros((TILE, wide), F32)
        for k in range(3):
            level = jnp.sum(jnp.where(line_wide == k, mixed, 0.0), axis=0, keepdims=True)
            extra += att_wide[k + 1] * level
        back[j, TILE:, :] += extra
        run = run + local_part[j] * here_scale

    def seed_copy(peer, slot):
        return pltpu.make_async_remote_copy(
            src_ref=back.at[peer],
            dst_ref=seeds.at[slot],
            send_sem=send3.at[peer],
            recv_sem=recv3.at[slot],
            device_id={"depth": in_group(peer)},
            device_id_type=MESH,
        )

    def total_copy(peer, slot):
        at = pl.ds(pl.multiple_of((slot % per_view) * wide, LANES), wide)
        return pltpu.make_async_remote_copy(
            src_ref=total_send,
            dst_ref=signal.at[slot // per_view, :, at],
            send_sem=send4.at[peer],
            recv_sem=recv4.at[slot],
            device_id={"depth": in_group(peer)},
            device_id_type=MESH,
        )

    for k in range(1, nc):
        seed_copy((c + k) % nc, c).start()
    seeds[c] = back[c]
    total_send[...] = counts
    signal[own_view, :, own_at] = counts
    for k in range(1, nc):
        total_copy((c + k) % nc, c).start()

    def clear(d, carry):
        zeros = jnp.zeros((3, TILE, LANES), F32)
        for v in range(views):
            spread_left[v, d, 0:3] = zeros
            spread_right[v, d, 0:3] = zeros
            spread_left[v, d, 3 + blocks : 5 + blocks] = zeros[:2]
            spread_right[v, d, 3 + blocks : 5 + blocks] = zeros[:2]
        return carry

    lax.fori_loop(0, depth, clear, 0)

    for k in range(1, nc):
        seed_copy((c + k) % nc, (c + k) % nc).wait_recv()

    def adjoint(chunk, carry):
        v, base = chunk // per_view, (chunk % per_view) * wide
        for part_at in range(0, wide, STEP):
            start = pl.multiple_of(base + part_at, STEP)
            at = pl.ds(start, STEP)
            factor = seeds[chunk, :TILE, part_at : part_at + STEP]
            constant = seeds[chunk, TILE:, part_at : part_at + STEP]
            direct = decay[v, :, at].reshape(depth, TILE, STEP) * factor[None]
            mixed = direct.reshape(depth * TILE, STEP) * field[v, :, at]
            corr[...] = dot3(adj_high, adj_low, mixed)

            def some(i, inner):
                shares = weight[v, pl.ds(pl.multiple_of(i * TILE, TILE), TILE), at]
                for row in range(TILE):
                    d = i * TILE + row
                    rows = pl.ds(pl.multiple_of(d * TILE, TILE), TILE)
                    value = decay[v, rows, at] * factor - corr[rows, :] - constant
                    right = value * jnp.broadcast_to(shares[row : row + 1], (TILE, STEP))
                    left = value - right
                    for j in range(STEP // LANES):
                        to = 3 + start // LANES + j
                        spread_left[v, d, to] = left[:, j * LANES : (j + 1) * LANES]
                        spread_right[v, d, to] = right[:, j * LANES : (j + 1) * LANES]
                return inner

            lax.fori_loop(0, depth // TILE, some, 0)
        return carry

    lax.fori_loop(0, nc, adjoint, 0)

    share_x = depth // nx
    share_z = share_x // nz

    def x_copy(peer, slot):
        return pltpu.make_async_remote_copy(
            src_ref=part.at[pl.ds(peer * share_x, share_x)],
            dst_ref=from_x.at[slot],
            send_sem=send5.at[peer],
            recv_sem=recv5.at[slot],
            device_id={"views": in_x(peer)},
            device_id_type=MESH,
        )

    def place(i, carry):
        peer = (x + 1 + i) % nx

        def place_row(r, inner):
            d = peer * share_x + r
            lefts = [None] * (blocks + 2)
            rights = [None] * (blocks + 2)
            for v in range(views):
                start = starts[v, d]
                block, rest = start >> 7, start & (LANES - 1)
                for ref, sums in ((spread_left, lefts), (spread_right, rights)):
                    turned = pltpu.roll(ref[v, d, pl.ds(2 - block, blocks + 3)], rest, 2)
                    for j in range(blocks + 2):
                        value = jnp.where(lane >= rest, turned[j + 1], turned[j])
                        sums[j] = value if v == 0 else sums[j] + value

            def total_of(value):
                return jnp.sum(value, axis=1, keepdims=True)

            low_left, low_right = total_of(lefts[0]), total_of(rights[0])
            top = lane == LANES - 1
            high_left = total_of(lefts[-1] + jnp.where(top, lefts[-2], 0.0))
            high_right = total_of(rights[-1])
            shifted = [pltpu.roll(rights[j + 1], 1, 1) for j in range(blocks)]
            for j in range(blocks):
                left = lefts[j + 1]
                if j == 0:
                    right = jnp.where(lane == 0, 0.0, shifted[0])
                    left = left + jnp.where(lane == 0, low_left, 0.0) + jnp.where(lane == 1, low_right, 0.0)
                else:
                    right = jnp.where(lane == 0, shifted[j - 1], shifted[j])
                if j == blocks - 1:
                    left = jnp.where(top, high_right + rights[-2], left)
                    left = left + jnp.where(lane == LANES - 2, high_left, 0.0)
                part[d, :, j * LANES : (j + 1) * LANES] = left + right
            return inner

        lax.fori_loop(0, share_x, place_row, 0)

        @pl.when(peer != x)
        def _():
            x_copy(peer, x).start()

        return carry

    lax.fori_loop(0, nx, place, 0)

    for k in range(1, nx):
        x_copy((x + k) % nx, (x + k) % nx).wait_recv()

    def reduced(r):
        value = part[x * share_x + r]
        for k in range(1, nx):
            value = value + from_x[(x + k) % nx, r]
        return value

    def z_copy(peer, slot):
        return pltpu.make_async_remote_copy(
            src_ref=z_out.at[peer],
            dst_ref=from_z.at[slot],
            send_sem=send6.at[peer],
            recv_sem=recv6.at[slot],
            device_id={"views": in_z(peer)},
            device_id_type=MESH,
        )

    for k in range(1, nz):
        peer = (zh + k) % nz

        def gather_z(r, carry):
            z_out[peer, r] = reduced(peer * share_z + r)
            return carry

        lax.fori_loop(0, share_z, gather_z, 0)
        z_copy(peer, zh).start()

    def own(r, carry):
        z_out[zh, r] = reduced(zh * share_z + r)
        return carry

    lax.fori_loop(0, share_z, own, 0)
    for k in range(1, nz):
        z_copy((zh + k) % nz, (zh + k) % nz).wait_recv()

    def finish(r, carry):
        value = z_out[zh, r]
        for k in range(1, nz):
            value = value + from_z[(zh + k) % nz, r]
        grad[x * share_x + zh * share_z + r] = value
        return carry

    lax.fori_loop(0, share_z, finish, 0)

    def piece(px, pz):
        return grad.at[pl.ds(px * share_x + pz * share_z, share_z)]

    def give_x(peer, px, pz):
        return pltpu.make_async_remote_copy(
            src_ref=piece(px, pz),
            dst_ref=piece(px, pz),
            send_sem=send7.at[peer, pz],
            recv_sem=recv7.at[px, pz],
            device_id={"views": in_x(peer)},
            device_id_type=MESH,
        )

    def give_z(peer, px, pz):
        return pltpu.make_async_remote_copy(
            src_ref=piece(px, pz),
            dst_ref=piece(px, pz),
            send_sem=send8.at[peer],
            recv_sem=recv7.at[px, pz],
            device_id={"views": in_z(peer)},
            device_id_type=MESH,
        )

    for k in range(1, nz):
        give_z((zh + k) % nz, x, zh).start()
    for k in range(1, nx):
        give_x((x + k) % nx, x, zh).start()
    for k in range(1, nz):
        pz = (zh + k) % nz
        give_z(pz, x, pz).wait_recv()
        for m in range(1, nx):
            give_x((x + m) % nx, x, pz).start()
    for k in range(nz):
        pz = (zh + k) % nz
        for m in range(1, nx):
            give_x((x + m) % nx, (x + m) % nx, pz).wait_recv()
    for k in range(1, nc):
        total_copy((c + k) % nc, (c + k) % nc).wait_recv()

    for k in range(1, nc):
        peer = (c + k) % nc
        to_group(peer).wait_send()
        seed_copy(peer, c).wait_send()
        total_copy(peer, c).wait_send()
    for k in range(1, ny):
        y_copy((y + k) % ny, y).wait_send()
    for k in range(1, nx):
        peer = (x + k) % nx
        x_copy(peer, x).wait_send()
        for pz in range(nz):
            give_x(peer, x, pz).wait_send()
    for k in range(1, nz):
        peer = (zh + k) % nz
        z_copy(peer, zh).wait_send()
        give_z(peer, x, zh).wait_send()


def body(sizes, concentration, shear_index, shear_weight, attenuation, yields, line_energy, measured):
    elements, rows, depth, width = concentration.shape
    views = shear_index.shape[0]
    nx, nz, ny, nc = sizes
    wide = views * width // nc
    blocks = width // LANES
    starts = shear_index[:, :, width // 2] - (width // 2 - LANES)
    smem = pl.BlockSpec(memory_space=pltpu.SMEM)
    vmem = pl.BlockSpec(memory_space=pltpu.VMEM)
    full = depth * elements

    def buf(*shape):
        return pltpu.VMEM(shape, F32)

    def sems(*shape):
        return pltpu.SemaphoreType.DMA(shape)

    gradient, signal = pl.pallas_call(
        functools.partial(kernel, sizes),
        out_shape=(
            jax.ShapeDtypeStruct((depth, elements, width), F32),
            jax.ShapeDtypeStruct((views, elements, width), F32),
        ),
        in_specs=[smem] * 4 + [vmem] * 3,
        out_specs=(vmem, vmem),
        scratch_shapes=[pltpu.VMEM((full, full), BF16)] * 4
        + [buf(depth, blocks + 3, elements, LANES)] * 2
        + [buf(views, full, width)] * 2
        + [buf(views, depth, blocks + 5, elements, LANES)] * 2
        + [
            buf(full, STEP),
            buf(nc, 2 * elements, wide),
            buf(nc, 2 * elements, wide),
            buf(nc, elements, wide),
            buf(nc, elements, wide),
            buf(2 * elements, wide),
            buf(ny, 2 * elements, wide),
            buf(ny, elements, wide),
            buf(nc, 2 * elements, wide),
            buf(nc, 2 * elements, wide),
            buf(elements, wide),
            buf(depth, elements, width),
            buf(nx, depth // nx, elements, width),
            buf(nz, depth // nx // nz, elements, width),
            buf(nz, depth // nx // nz, elements, width),
        ]
        + [sems(nc)] * 2
        + [sems(ny)] * 2
        + [sems(nc)] * 4
        + [sems(nx)] * 2
        + [sems(nz)] * 2
        + [sems(nx, nz)] * 2
        + [sems(nz)],
        compiler_params=pltpu.CompilerParams(
            collective_id=0, has_side_effects=True, vmem_limit_bytes=44 * 1024 * 1024
        ),
    )(
        starts,
        attenuation,
        yields,
        line_energy,
        concentration.reshape(elements, depth, width),
        shear_weight,
        measured.reshape(views, elements, width),
    )
    gradient = jnp.transpose(gradient, (1, 0, 2)).reshape(elements, rows, depth, width)
    return gradient, signal.reshape(views, elements, rows, width)


SIZES = {(8, 64): (4, 2, 8, 8)}


def solution(mesh):
    sizes = SIZES[mesh.shape["views"], mesh.shape["depth"]]
    return jax.shard_map(
        functools.partial(body, sizes),
        mesh=mesh,
        in_specs=(
            P(None, None, "depth", None),
            P("views", "depth", None),
            P("views", "depth", None),
            P(),
            P(),
            P(),
            P("views", None, None, None),
        ),
        out_specs=(P(None, None, "depth", None), P("views", None, None, None)),
        check_vma=False,
    )
```

time: 1630 us -> 84.5 us (0.05); the launches traced: 1610 us -> 83.6 us
  waiting for transfers between devices: 692 us -> 0 us
  local copies, waits for them, and re-layouts: 542 us -> 5.97 us
  blocking collectives: 170 us -> 0 us
  other arithmetic: 170 us -> 0.87 us
  Pallas kernels: 0 us -> 76 us
    psum x2 -> x0, waiting for transfers between devices: 591 us -> none  [the longest x1 460 us: body(): signal = lax.psum(jnp.sum(emitted, axis=3), 'depth')]
    gather x579 -> x0, local copies, waits for them, and re-layouts: 516 us -> none
    all_gather x2 -> x0, blocking collectives: 170 us -> none  [carried_in(): everything = lax.all_gather(value, axis)]
    select_n x257 -> x0, other arithmetic: 148 us -> none  [the longest x256 148 us: turn(): return jnp.where(reached, new, before)]
    all_gather x2 -> x0, waiting for transfers between devices: 101 us -> none  [carried_in(): everything = lax.all_gather(value, axis)]
    pallas_call x0 -> x1, Pallas kernels: none -> 76 us  [body(): pl.pallas_call(functools.partial(kernel, sizes), out_shape=(jax.ShapeDtyp...]
  transfers between devices with their start and end apart: 4 -> 0, of which waited for: 4 -> 0; matrix products, arithmetic and copies ran while one was open for 3% -> 0% of each run, Pallas kernels for 0% -> 0%
where the time goes in v1:
time: 84.5 us; the launch traced here: 83.6 us
  Pallas kernels  76 us (90%)
  local copies, waits for them, and re-layouts  5.97 us (7%)
  other arithmetic  0.87 us (1%)
    pallas_call x1, Pallas kernels, body(): pl.pallas_call(functools.partial(kernel, sizes), out_shape=(jax.ShapeDtyp...  76 us
    unnamed x13, local copies, waits for them, and re-layouts  5.97 us

profile of v1, /device:TPU:1, one launch (start us, length us, event | category | flops | bytes accessed | tf_op | source)
XLA Modules:
  0.0 83.6 jit_solution(7097358851028305813)
XLA Ops:
  0.6 0.9 %add_reduce_fusion.starts = s32[2,32]{1,0:T(2,128)S(1)} fusion(s32[2,32,1024]{2,1,0:T(8,128)} %param.8), kind=kLoop, calls=%fused_computation.1 | loop fusion | flops 64 | bytes 512 | tf_op jit(solution)/shard_map/sub | solution.py:595
  1.5 0.0 copy-start.2
  1.5 0.9 %copy.15 = f32[2,8,1,1024]{3,1,2,0:T(8,128)S(1)} copy(f32[2,8,1,1024]{3,2,1,0:T(1,128)} %param.13) | data formatting | bytes 131072
  2.4 0.0 copy-start.3
  2.4 0.0 copy-start.4
  2.4 0.0 copy-done.2
  2.4 0.6 copy-done.3
  3.0 0.0 copy-done.4
  3.1 0.0 copy-start
  3.1 1.2 %copy-done = f32[8,1,32,1024]{3,2,1,0:T(8,128)S(1)} copy-done((f32[8,1,32,1024]{3,2,1,0:T(8,128)S(1)}, f32[8,1,32,1024]{3,2,1,0:T(8,128)}, u32[]{:S(2)}) %copy-start) | copy-done | bytes 1048600
  4.3 0.0 copy-start.1
  4.3 0.9 %copy-done.1 = f32[2,32,1024]{2,1,0:T(8,128)S(1)} copy-done((f32[2,32,1024]{2,1,0:T(8,128)S(1)}, f32[2,32,1024]{2,1,0:T(8,128)}, u32[]{:S(2)}) %copy-start.1) | copy-done | bytes 262168
  5.2 76.0 %shard_map.86 = (f32[32,8,1024]{2,1,0:T(8,128)S(1)}, f32[2,8,1024]{2,1,0:T(8,128)S(1)}) custom-call(s32[2,32]{1,0:T(2,128)S(1)} %add_reduce_fusion.starts, f32[4,8]{1,0:T(4,128)S(1)} %copy-done.2, f32[8]{0:T(128)S(1)} %copy-done.3, s32[8]{0:T(128)S(1)} %copy-done.4, f32[8,32,1024]{2,1,0:T(8,128)S(1)} %bitcast.8, f32[2,32,1024]{2,1,0:T(8,128)S(1)} %copy-done.1, ...), custom_call_target="tpu_custom_call" | custom-call | tf_op jit(solution)/shard_map/pallas_call | solution.py:606
  81.3 1.6 %copy.11 = f32[8,1,32,1024]{3,2,1,0:T(8,128)} copy(f32[8,1,32,1024]{3,0,2,1:T(8,128)S(1)} %bitcast.9) | data formatting | bytes 2097152
  82.9 0.7 copy.12
Async XLA Ops:
  1.5 0.9 %copy-start.2 = (f32[4,8]{1,0:T(4,128)S(1)}, f32[4,8]{1,0:T(4,128)}, u32[]{:S(2)}) copy-start(f32[4,8]{1,0:T(4,128)} %att.1) | copy-start | bytes 388
  2.4 0.7 copy-start.3
  2.4 0.7 copy-start.4
  3.1 1.2 %copy-start = (f32[8,1,32,1024]{3,2,1,0:T(8,128)S(1)}, f32[8,1,32,1024]{3,2,1,0:T(8,128)}, u32[]{:S(2)}) copy-start(f32[8,1,32,1024]{3,2,1,0:T(8,128)} %param.7) | copy-start | bytes 3145732
  4.3 0.9 %copy-start.1 = (f32[2,32,1024]{2,1,0:T(8,128)S(1)}, f32[2,32,1024]{2,1,0:T(8,128)}, u32[]{:S(2)}) copy-start(f32[2,32,1024]{2,1,0:T(8,128)} %weight.1) | copy-start | bytes 786436

commit v2 on v1

--- a/solution.py
+++ b/solution.py
@@ -10,6 +10,7 @@
 LANES = 128
 TILE = 8
 STEP = 256
+PAIR = 2
 MESH = pl.DeviceIdType.MESH
 F32 = jnp.float32
 BF16 = jnp.bfloat16
@@ -31,15 +32,23 @@
 
 def kernel(
     sizes,
-    starts,
+    index_in,
+    att_in,
+    yields_in,
+    line_in,
+    conc_in,
+    weight_in,
+    measured_in,
+    grad,
+    signal,
+    shifts,
     att,
     yields,
     line,
     conc,
     weight,
     measured,
-    grad,
-    signal,
+    fetched,
     mat_high,
     mat_low,
     adj_high,
@@ -103,6 +112,29 @@
     def in_z(k):
         return x * nz + k
 
+    own_view, own_base = c // per_view, pl.multiple_of((c % per_view) * wide, LANES)
+    own_at = pl.ds(own_base, wide)
+    middle = width // 2
+    fetches = [
+        pltpu.make_async_copy(src, dst, fetched.at[i])
+        for i, (src, dst) in enumerate(
+            [
+                (conc_in, conc),
+                (weight_in, weight),
+                (index_in.at[:, :, middle : middle + LANES], shifts),
+                (att_in, att),
+                (yields_in, yields),
+                (line_in, line),
+            ]
+            + [(measured_in.at[own_view, e, :, own_at], measured.at[e]) for e in range(TILE)]
+        )
+    ]
+    for fetch in fetches:
+        fetch.start()
+
+    def start_of(v, d):
+        return jnp.clip(shifts[v, d, 0] - (middle - LANES), 0, 2 * LANES)
+
     barrier = pltpu.get_barrier_semaphore()
     greeted = 0
     for k in range(1, nc):
@@ -118,6 +150,9 @@
         pl.semaphore_signal(barrier, inc=1, device_id={"views": in_z((zh + k) % nz)}, device_id_type=MESH)
         greeted += 1
 
+    for fetch in fetches[3:6]:
+        fetch.wait()
+
     rows16 = lax.broadcasted_iota(jnp.int32, (2 * TILE, depth * TILE), 0)
     cols16 = lax.broadcasted_iota(jnp.int32, (2 * TILE, depth * TILE), 1)
     row_item, col_item, col_depth = rows16 & (TILE - 1), cols16 & (TILE - 1), cols16 // TILE
@@ -154,6 +189,8 @@
 
     lane = lax.broadcasted_iota(jnp.int32, (TILE, LANES), 1)
     sub = lax.broadcasted_iota(jnp.int32, (TILE, LANES), 0)
+
+    fetches[0].wait()
 
     def turn_rows(i, carry):
         at = pl.ds(pl.multiple_of(i * TILE, TILE), TILE)
@@ -189,12 +226,15 @@
             pad_step[d, j] = last - before_last
         return carry
 
-    lax.fori_loop(0, depth, pad_row, 0, unroll=2)
+    lax.fori_loop(0, depth, pad_row, 0, unroll=4)
+
+    for fetch in fetches[1:3]:
+        fetch.wait()
 
     for v in range(views):
 
         def take_row(d, row, shares, sums):
-            start = starts[v, d]
+            start = start_of(v, d)
             block, rest = start >> 7, start & (LANES - 1)
             turn = (LANES - rest) & (LANES - 1)
             left = pltpu.roll(pad_left[d, pl.ds(block, blocks + 1)], turn, 2)
@@ -238,8 +278,7 @@
             device_id_type=MESH,
         )
 
-    def emit(i, carry):
-        chunk = (c + 1 + i) % nc
+    def emit_chunk(chunk):
         v, base = chunk // per_view, (chunk % per_view) * wide
         for part_at in range(0, wide, STEP):
             at = pl.ds(pl.multiple_of(base + part_at, STEP), STEP)
@@ -249,13 +288,19 @@
             value = (value * values).reshape(depth, TILE, STEP)
             slab[chunk, :TILE, part_at : part_at + STEP] = jnp.sum(value, axis=0) * over(yield_tile, STEP)
 
-        @pl.when(chunk != c)
-        def _():
-            to_group(chunk).start()
+    def emit(i, carry):
+        chunks = [(c + 1 + PAIR * i + k) % nc for k in range(PAIR)]
+        for chunk in chunks:
+            emit_chunk(chunk)
+        for chunk in chunks:
+
+            @pl.when(chunk != c)
+            def _():
+                to_group(chunk).start()
 
         return carry
 
-    lax.fori_loop(0, nc, emit, 0)
+    lax.fori_loop(0, nc // PAIR, emit, 0)
     group[c] = slab[c]
 
     def from_group(k):
@@ -328,10 +373,10 @@
         total += piece
         prior += jnp.where(j < y, piece, 0.0)
         following += jnp.where(j > y, piece, 0.0)
-    own_view, own_base = c // per_view, pl.multiple_of((c % per_view) * wide, LANES)
-    own_at = pl.ds(own_base, wide)
+    for fetch in fetches[6:]:
+        fetch.wait()
     counts = total * (1.0 / depth_total)
-    misfit = counts - measured[own_view, :, own_at]
+    misfit = counts - jnp.concatenate([measured[e] for e in range(TILE)], axis=0)
     here_scale = group_scale[y]
     run = following
     for j in reversed(range(nc)):
@@ -393,7 +438,7 @@
     for k in range(1, nc):
         seed_copy((c + k) % nc, (c + k) % nc).wait_recv()
 
-    def adjoint(chunk, carry):
+    def adjoint_chunk(chunk, corr):
         v, base = chunk // per_view, (chunk % per_view) * wide
         for part_at in range(0, wide, STEP):
             start = pl.multiple_of(base + part_at, STEP)
@@ -403,51 +448,52 @@
             direct = decay[v, :, at].reshape(depth, TILE, STEP) * factor[None]
             mixed = direct.reshape(depth * TILE, STEP) * field[v, :, at]
             corr[...] = dot3(adj_high, adj_low, mixed)
-
-            def some(i, inner):
-                shares = weight[v, pl.ds(pl.multiple_of(i * TILE, TILE), TILE), at]
-                for row in range(TILE):
-                    d = i * TILE + row
-                    rows = pl.ds(pl.multiple_of(d * TILE, TILE), TILE)
-                    value = decay[v, rows, at] * factor - corr[rows, :] - constant
-                    right = value * jnp.broadcast_to(shares[row : row + 1], (TILE, STEP))
-                    left = value - right
-                    for j in range(STEP // LANES):
-                        to = 3 + start // LANES + j
-                        spread_left[v, d, to] = left[:, j * LANES : (j + 1) * LANES]
-                        spread_right[v, d, to] = right[:, j * LANES : (j + 1) * LANES]
-                return inner
-
-            lax.fori_loop(0, depth // TILE, some, 0)
+            for d in range(depth):
+                if d % TILE == 0:
+                    shares = weight[v, d : d + TILE, at]
+                rows = slice(d * TILE, (d + 1) * TILE)
+                value = decay[v, rows, at] * factor - corr[rows, :] - constant
+                right = value * jnp.broadcast_to(shares[d % TILE : d % TILE + 1], (TILE, STEP))
+                left = value - right
+                rest = start_of(v, d) & (LANES - 1)
+                for j in range(STEP // LANES):
+                    to = 3 + start // LANES + j
+                    spread_left[v, d, to] = pltpu.roll(left[:, j * LANES : (j + 1) * LANES], rest, 1)
+                    spread_right[v, d, to] = pltpu.roll(right[:, j * LANES : (j + 1) * LANES], rest, 1)
+
+    def adjoint(i, carry):
+        for k in range(PAIR):
+            adjoint_chunk(PAIR * i + k, corr.at[k])
         return carry
 
-    lax.fori_loop(0, nc, adjoint, 0)
+    lax.fori_loop(0, nc // PAIR, adjoint, 0)
 
     share_x = depth // nx
     share_z = share_x // nz
 
-    def x_copy(peer, slot):
-        return pltpu.make_async_remote_copy(
-            src_ref=part.at[pl.ds(peer * share_x, share_x)],
-            dst_ref=from_x.at[slot],
-            send_sem=send5.at[peer],
-            recv_sem=recv5.at[slot],
+    def x_copy(peer, pz, slot):
+        return pltpu.make_async_remote_copy(
+            src_ref=part.at[pl.ds(peer * share_x + pz * share_z, share_z)],
+            dst_ref=from_x.at[slot, pz],
+            send_sem=send5.at[peer, pz],
+            recv_sem=recv5.at[slot, pz],
             device_id={"views": in_x(peer)},
             device_id_type=MESH,
         )
 
     def place(i, carry):
-        peer = (x + 1 + i) % nx
-
-        def place_row(r, inner):
-            d = peer * share_x + r
+        peer, pz = (x + 1 + i % nx) % nx, (zh + 1 + i // nx) % nz
+        first_row = peer * share_x + pz * share_z
+
+        for r in range(share_z):
+            d = first_row + r
             lefts = [None] * (blocks + 2)
             rights = [None] * (blocks + 2)
             for v in range(views):
-                start = starts[v, d]
+                start = start_of(v, d)
                 block, rest = start >> 7, start & (LANES - 1)
                 for ref, sums in ((spread_left, lefts), (spread_right, rights)):
-                    turned = pltpu.roll(ref[v, d, pl.ds(2 - block, blocks + 3)], rest, 2)
+                    turned = ref[v, d, pl.ds(2 - block, blocks + 3)]
                     for j in range(blocks + 2):
                         value = jnp.where(lane >= rest, turned[j + 1], turned[j])
                         sums[j] = value if v == 0 else sums[j] + value
@@ -471,25 +517,23 @@
                     left = jnp.where(top, high_right + rights[-2], left)
                     left = left + jnp.where(lane == LANES - 2, high_left, 0.0)
                 part[d, :, j * LANES : (j + 1) * LANES] = left + right
-            return inner
-
-        lax.fori_loop(0, share_x, place_row, 0)
 
         @pl.when(peer != x)
         def _():
-            x_copy(peer, x).start()
+            x_copy(peer, pz, x).start()
 
         return carry
 
-    lax.fori_loop(0, nx, place, 0)
-
-    for k in range(1, nx):
-        x_copy((x + k) % nx, (x + k) % nx).wait_recv()
-
-    def reduced(r):
-        value = part[x * share_x + r]
+    lax.fori_loop(0, nx * nz, place, 0)
+
+    def arrived(pz):
         for k in range(1, nx):
-            value = value + from_x[(x + k) % nx, r]
+            x_copy((x + k) % nx, pz, (x + k) % nx).wait_recv()
+
+    def reduced(pz, r):
+        value = part[x * share_x + pz * share_z + r]
+        for k in range(1, nx):
+            value = value + from_x[(x + k) % nx, pz, r]
         return value
 
     def z_copy(peer, slot):
@@ -504,16 +548,19 @@
 
     for k in range(1, nz):
         peer = (zh + k) % nz
+        arrived(peer)
 
         def gather_z(r, carry):
-            z_out[peer, r] = reduced(peer * share_z + r)
+            z_out[peer, r] = reduced(peer, r)
             return carry
 
         lax.fori_loop(0, share_z, gather_z, 0)
         z_copy(peer, zh).start()
 
+    arrived(zh)
+
     def own(r, carry):
-        z_out[zh, r] = reduced(zh * share_z + r)
+        z_out[zh, r] = reduced(zh, r)
         return carry
 
     lax.fori_loop(0, share_z, own, 0)
@@ -577,8 +624,8 @@
         y_copy((y + k) % ny, y).wait_send()
     for k in range(1, nx):
         peer = (x + k) % nx
-        x_copy(peer, x).wait_send()
         for pz in range(nz):
+            x_copy(peer, pz, x).wait_send()
             give_x(peer, x, pz).wait_send()
     for k in range(1, nz):
         peer = (zh + k) % nz
@@ -592,8 +639,7 @@
     nx, nz, ny, nc = sizes
     wide = views * width // nc
     blocks = width // LANES
-    starts = shear_index[:, :, width // 2] - (width // 2 - LANES)
-    smem = pl.BlockSpec(memory_space=pltpu.SMEM)
+    hbm = pl.BlockSpec(memory_space=pltpu.HBM)
     vmem = pl.BlockSpec(memory_space=pltpu.VMEM)
     full = depth * elements
 
@@ -606,17 +652,27 @@
     gradient, signal = pl.pallas_call(
         functools.partial(kernel, sizes),
         out_shape=(
-            jax.ShapeDtypeStruct((depth, elements, width), F32),
-            jax.ShapeDtypeStruct((views, elements, width), F32),
+            pltpu.VMEM((depth, elements, width), F32),
+            pltpu.VMEM((views, elements, width), F32),
         ),
-        in_specs=[smem] * 4 + [vmem] * 3,
+        in_specs=[hbm] * 7,
         out_specs=(vmem, vmem),
-        scratch_shapes=[pltpu.VMEM((full, full), BF16)] * 4
+        scratch_shapes=[
+            pltpu.SMEM((views, depth, LANES), jnp.int32),
+            pltpu.SMEM(attenuation.shape, F32),
+            pltpu.SMEM(yields.shape, F32),
+            pltpu.SMEM(line_energy.shape, jnp.int32),
+            buf(elements, depth, width),
+            buf(views, depth, width),
+            buf(elements, rows, wide),
+            sems(6 + elements),
+        ]
+        + [pltpu.VMEM((full, full), BF16)] * 4
         + [buf(depth, blocks + 3, elements, LANES)] * 2
         + [buf(views, full, width)] * 2
         + [buf(views, depth, blocks + 5, elements, LANES)] * 2
         + [
-            buf(full, STEP),
+            buf(PAIR, full, STEP),
             buf(nc, 2 * elements, wide),
             buf(nc, 2 * elements, wide),
             buf(nc, elements, wide),
@@ -628,28 +684,28 @@
             buf(nc, 2 * elements, wide),
             buf(elements, wide),
             buf(depth, elements, width),
-            buf(nx, depth // nx, elements, width),
+            buf(nx, nz, depth // nx // nz, elements, width),
             buf(nz, depth // nx // nz, elements, width),
             buf(nz, depth // nx // nz, elements, width),
         ]
         + [sems(nc)] * 2
         + [sems(ny)] * 2
         + [sems(nc)] * 4
-        + [sems(nx)] * 2
+        + [sems(nx, nz)] * 2
         + [sems(nz)] * 2
         + [sems(nx, nz)] * 2
         + [sems(nz)],
         compiler_params=pltpu.CompilerParams(
-            collective_id=0, has_side_effects=True, vmem_limit_bytes=44 * 1024 * 1024
+            collective_id=0, has_side_effects=True, vmem_limit_bytes=56 * 1024 * 1024
         ),
     )(
-        starts,
+        shear_index,
         attenuation,
         yields,
         line_energy,
         concentration.reshape(elements, depth, width),
         shear_weight,
-        measured.reshape(views, elements, width),
+        measured,
     )
     gradient = jnp.transpose(gradient, (1, 0, 2)).reshape(elements, rows, depth, width)
     return gradient, signal.reshape(views, elements, rows, width)

time: 84.5 us -> 68.7 us (0.81)
  Pallas kernels: 76 us -> 65.6 us
  local copies, waits for them, and re-layouts: 5.97 us -> 2.28 us
  other arithmetic: 0.87 us -> 0 us
    pallas_call x1, Pallas kernels: 76 us -> 65.6 us  [body(): pl.pallas_call(functools.partial(kernel, sizes), out_shape=(pltpu.VMEM((d...]
    unnamed x13 -> x2, local copies, waits for them, and re-layouts: 5.97 us -> 2.28 us
    sub x1 -> x0, other arithmetic: 0.87 us -> none  [body(): starts = shear_index[:, :, width // 2] - (width // 2 - LANES)]
where the time goes in v2:
time: 68.7 us; the launch traced here: 68.6 us
  Pallas kernels  65.6 us (95%)
  local copies, waits for them, and re-layouts  2.28 us (3%)
    pallas_call x1, Pallas kernels, body(): pl.pallas_call(functools.partial(kernel, sizes), out_shape=(pltpu.VMEM((d...  65.6 us
    unnamed x2, local copies, waits for them, and re-layouts  2.28 us

profile of v2, /device:TPU:1, one launch (start us, length us, event | category | flops | bytes accessed | tf_op | source)
XLA Modules:
  0.0 68.6 jit_solution(2296319217583213498)
XLA Ops:
  0.6 65.6 %shard_map.86 = (f32[32,8,1024]{2,1,0:T(8,128)S(1)}, f32[2,8,1024]{2,1,0:T(8,128)S(1)}) custom-call(s32[2,32,1024]{2,1,0:T(8,128)} %index_in.1, f32[4,8]{1,0:T(4,128)} %att_in.1, f32[8]{0:T(128)} %yields_in.1, s32[8]{0:T(128)} %line_in.1, f32[8,32,1024]{2,1,0:T(8,128)} %bitcast.7, f32[2,32,1024]{2,1,0:T(8,128)} %weight_in.1, f32[2,8,1,1024]{3,2,1,0:T(1,128)} %measured_in.1), custom_call_target="tpu_custom_call" | custom-call | tf_op jit(solution)/shard_map/pallas_call | solution.py:652
  66.3 1.6 %copy.9 = f32[8,1,32,1024]{3,2,1,0:T(8,128)} copy(f32[8,1,32,1024]{3,0,2,1:T(8,128)S(1)} %bitcast.5) | data formatting | bytes 2097152
  67.9 0.7 %copy.10 = f32[2,8,1,1024]{3,2,1,0:T(1,128)} copy(f32[2,8,1,1024]{3,1,0,2:T(8,128)S(1)} %bitcast.6) | data formatting | bytes 131072

commit v3 on v2

--- a/solution.py
+++ b/solution.py
@@ -11,6 +11,7 @@
 TILE = 8
 STEP = 256
 PAIR = 2
+SPLIT = 4
 MESH = pl.DeviceIdType.MESH
 F32 = jnp.float32
 BF16 = jnp.bfloat16
@@ -95,10 +96,15 @@
     blocks = width // LANES
     wide = views * width // nc
     per_view = width // wide
+    tiles = wide // LANES
     depth_total = depth * ny * nc
     vi, di = lax.axis_index("views"), lax.axis_index("depth")
     x, zh = vi // nz, vi % nz
     y, c = di // nc, di % nc
+
+    def flip(k):
+        bits = [((c // b + k // b) % 2) * b for b in (1, 2, 4) if b < nc]
+        return sum(bits)
 
     def in_group(k):
         return y * nc + k
@@ -189,6 +195,19 @@
 
     lane = lax.broadcasted_iota(jnp.int32, (TILE, LANES), 1)
     sub = lax.broadcasted_iota(jnp.int32, (TILE, LANES), 0)
+
+    def stack_rows(levels):
+        result = jnp.broadcast_to(levels[0], (TILE, LANES))
+        for k in range(1, TILE):
+            result = jnp.where(sub == k, jnp.broadcast_to(levels[k], (TILE, LANES)), result)
+        return result
+
+    def columns_of(ref, j):
+        return jnp.concatenate([ref[j, b] for b in range(tiles)], axis=1)
+
+    def packed_row(ref, j, b, k):
+        at = 4 * (b % 2) + k
+        return jnp.broadcast_to(ref[j, tiles + b // 2, at : at + 1, :], (TILE, LANES))
 
     fetches[0].wait()
 
@@ -258,13 +277,12 @@
 
         zero = jnp.zeros((TILE, LANES), F32)
         sums = lax.fori_loop(0, depth // TILE, take_rows, (zero,) * blocks)
-        for j in range(blocks):
-            chunk, offset = divmod((v * width + j * LANES), wide)
-            absorbed = jnp.zeros((TILE, LANES), F32)
-            for k in range(4):
-                level = jnp.sum(att_tile[k] * sums[j], axis=0, keepdims=True)
-                absorbed = jnp.where(sub == k, jnp.broadcast_to(level, (TILE, LANES)), absorbed)
-            slab[chunk, TILE:, offset : offset + LANES] = absorbed
+        for j in range(0, blocks, 2):
+            chunk, offset = divmod(v * blocks + j, tiles)
+            levels = [
+                jnp.sum(att_tile[k] * sums[j + h], axis=0, keepdims=True) for h in range(2) for k in range(4)
+            ]
+            slab[chunk, tiles + offset // 2] = stack_rows(levels)
 
     pl.semaphore_wait(barrier, greeted)
 
@@ -286,10 +304,12 @@
             value = jnp.exp(-dot3(mat_high, mat_low, values))
             decay[v, :, at] = value
             value = (value * values).reshape(depth, TILE, STEP)
-            slab[chunk, :TILE, part_at : part_at + STEP] = jnp.sum(value, axis=0) * over(yield_tile, STEP)
+            value = jnp.sum(value, axis=0)
+            for j in range(STEP // LANES):
+                slab[chunk, part_at // LANES + j] = value[:, j * LANES : (j + 1) * LANES] * yield_tile
 
     def emit(i, carry):
-        chunks = [(c + 1 + PAIR * i + k) % nc for k in range(PAIR)]
+        chunks = [flip(nc - PAIR * (i + 1) + k) for k in range(PAIR)]
         for chunk in chunks:
             emit_chunk(chunk)
         for chunk in chunks:
@@ -317,12 +337,13 @@
         from_group((c + k) % nc).wait_recv()
 
     line_wide = over(line_tile, wide)
-    att_wide = [over(tile, wide) for tile in att_tile]
 
     def scales(ref, count):
         first, later = [], []
         for j in range(count):
-            levels = [jnp.broadcast_to(ref[j, TILE + k : TILE + k + 1, :], (TILE, wide)) for k in range(4)]
+            levels = [
+                jnp.concatenate([packed_row(ref, j, b, k) for b in range(tiles)], axis=1) for k in range(4)
+            ]
             first.append(levels[0])
             later.append(pick(line_wide, levels[1:]))
         after = [None] * count
@@ -338,15 +359,18 @@
         return result
 
     emitted_sum = jnp.zeros((TILE, wide), F32)
-    absorbed_sum = jnp.zeros((TILE, wide), F32)
     for j, scale in enumerate(scales(group, nc)):
-        piece = group[j, :TILE, :] * scale
+        piece = columns_of(group, j) * scale
         local_scale[j] = scale
         local_part[j] = piece
         emitted_sum += piece
-        absorbed_sum += group[j, TILE:, :]
-    group_send[:TILE, :] = emitted_sum
-    group_send[TILE:, :] = absorbed_sum
+    for b in range(tiles):
+        group_send[b] = emitted_sum[:, b * LANES : (b + 1) * LANES]
+    for b in range(tiles, tiles + tiles // 2):
+        value = group[0, b]
+        for j in range(1, nc):
+            value = value + group[j, b]
+        group_send[b] = value
 
     def y_copy(peer, slot):
         return pltpu.make_async_remote_copy(
@@ -358,7 +382,7 @@
             device_id_type=MESH,
         )
 
-    for k in range(1, ny):
+    for k in sorted(range(1, ny), key=lambda k: -min(k, ny - k)):
         y_copy((y + k) % ny, y).start()
     group_recv[y] = group_send[...]
     for k in range(1, ny):
@@ -368,7 +392,7 @@
     prior = jnp.zeros((TILE, wide), F32)
     following = jnp.zeros((TILE, wide), F32)
     for j, scale in enumerate(scales(group_recv, ny)):
-        piece = group_recv[j, :TILE, :] * scale
+        piece = columns_of(group_recv, j) * scale
         group_scale[j] = scale
         total += piece
         prior += jnp.where(j < y, piece, 0.0)
@@ -378,21 +402,25 @@
     counts = total * (1.0 / depth_total)
     misfit = counts - jnp.concatenate([measured[e] for e in range(TILE)], axis=0)
     here_scale = group_scale[y]
+    later = [None] * nc
     run = following
     for j in reversed(range(nc)):
-        level = jnp.sum(misfit * run, axis=0, keepdims=True)
-        back[j, TILE:, :] = att_wide[0] * level
+        later[j] = jnp.sum(misfit * run, axis=0, keepdims=True)
         run = run + local_part[j] * here_scale
     run = prior
     yield_wide = over(yield_tile, wide)
     for j in range(nc):
-        back[j, :TILE, :] = misfit * yield_wide * local_scale[j] * here_scale
+        value = misfit * yield_wide * local_scale[j] * here_scale
+        for b in range(tiles):
+            back[j, b] = value[:, b * LANES : (b + 1) * LANES]
         mixed = misfit * run
-        extra = jnp.zeros((TILE, wide), F32)
-        for k in range(3):
-            level = jnp.sum(jnp.where(line_wide == k, mixed, 0.0), axis=0, keepdims=True)
-            extra += att_wide[k + 1] * level
-        back[j, TILE:, :] += extra
+        levels = [later[j]] + [
+            jnp.sum(jnp.where(line_wide == k, mixed, 0.0), axis=0, keepdims=True) for k in range(3)
+        ]
+        for b in range(0, tiles, 2):
+            back[j, tiles + b // 2] = stack_rows(
+                [level[:, (b + h) * LANES : (b + h + 1) * LANES] for h in range(2) for level in levels]
+            )
         run = run + local_part[j] * here_scale
 
     def seed_copy(peer, slot):
@@ -409,18 +437,19 @@
         at = pl.ds(pl.multiple_of((slot % per_view) * wide, LANES), wide)
         return pltpu.make_async_remote_copy(
             src_ref=total_send,
-            dst_ref=signal.at[slot // per_view, :, at],
+            dst_ref=signal.at[slot // per_view, :, :, at],
             send_sem=send4.at[peer],
             recv_sem=recv4.at[slot],
             device_id={"depth": in_group(peer)},
             device_id_type=MESH,
         )
 
-    for k in range(1, nc):
-        seed_copy((c + k) % nc, c).start()
+    for k in reversed(range(1, nc)):
+        seed_copy(flip(k), c).start()
     seeds[c] = back[c]
-    total_send[...] = counts
-    signal[own_view, :, own_at] = counts
+    for e in range(TILE):
+        total_send[e] = counts[e : e + 1]
+        signal[own_view, e, :, own_at] = counts[e : e + 1]
     for k in range(1, nc):
         total_copy((c + k) % nc, c).start()
 
@@ -435,16 +464,16 @@
 
     lax.fori_loop(0, depth, clear, 0)
 
-    for k in range(1, nc):
-        seed_copy((c + k) % nc, (c + k) % nc).wait_recv()
-
     def adjoint_chunk(chunk, corr):
         v, base = chunk // per_view, (chunk % per_view) * wide
         for part_at in range(0, wide, STEP):
             start = pl.multiple_of(base + part_at, STEP)
             at = pl.ds(start, STEP)
-            factor = seeds[chunk, :TILE, part_at : part_at + STEP]
-            constant = seeds[chunk, TILE:, part_at : part_at + STEP]
+            here = range(part_at // LANES, (part_at + STEP) // LANES)
+            factor = jnp.concatenate([seeds[chunk, b] for b in here], axis=1)
+            constant = jnp.concatenate(
+                [sum(att_tile[k] * packed_row(seeds, chunk, b, k) for k in range(4)) for b in here], axis=1
+            )
             direct = decay[v, :, at].reshape(depth, TILE, STEP) * factor[None]
             mixed = direct.reshape(depth * TILE, STEP) * field[v, :, at]
             corr[...] = dot3(adj_high, adj_low, mixed)
@@ -462,31 +491,39 @@
                     spread_right[v, d, to] = pltpu.roll(right[:, j * LANES : (j + 1) * LANES], rest, 1)
 
     def adjoint(i, carry):
-        for k in range(PAIR):
-            adjoint_chunk(PAIR * i + k, corr.at[k])
+        chunks = [flip(PAIR * i + k) for k in range(PAIR)]
+        for chunk in chunks:
+
+            @pl.when(chunk != c)
+            def _():
+                seed_copy(chunk, chunk).wait_recv()
+
+        for k, chunk in enumerate(chunks):
+            adjoint_chunk(chunk, corr.at[k])
         return carry
 
     lax.fori_loop(0, nc // PAIR, adjoint, 0)
 
     share_x = depth // nx
     share_z = share_x // nz
-
-    def x_copy(peer, pz, slot):
-        return pltpu.make_async_remote_copy(
-            src_ref=part.at[pl.ds(peer * share_x + pz * share_z, share_z)],
-            dst_ref=from_x.at[slot, pz],
-            send_sem=send5.at[peer, pz],
-            recv_sem=recv5.at[slot, pz],
+    share = share_z // SPLIT
+
+    def row_of(px, pz, s):
+        return px * share_x + pz * share_z + s * share
+
+    def x_copy(peer, pz, s, slot):
+        return pltpu.make_async_remote_copy(
+            src_ref=part.at[pl.ds(row_of(peer, pz, s), share)],
+            dst_ref=from_x.at[slot, pz, s],
+            send_sem=send5.at[peer, pz, s],
+            recv_sem=recv5.at[slot, pz, s],
             device_id={"views": in_x(peer)},
             device_id_type=MESH,
         )
 
     def place(i, carry):
-        peer, pz = (x + 1 + i % nx) % nx, (zh + 1 + i // nx) % nz
-        first_row = peer * share_x + pz * share_z
-
-        for r in range(share_z):
-            d = first_row + r
+        pz, s = (zh + 1 + i // SPLIT) % nz, i % SPLIT
+        for d in [row_of((x + 1 + k) % nx, pz, s) + r for k in range(nx) for r in range(share)]:
             lefts = [None] * (blocks + 2)
             rights = [None] * (blocks + 2)
             for v in range(views):
@@ -518,100 +555,107 @@
                     left = left + jnp.where(lane == LANES - 2, high_left, 0.0)
                 part[d, :, j * LANES : (j + 1) * LANES] = left + right
 
-        @pl.when(peer != x)
-        def _():
-            x_copy(peer, pz, x).start()
-
+        for k in range(1, nx):
+            x_copy((x + k) % nx, pz, s, x).start()
         return carry
 
-    lax.fori_loop(0, nx * nz, place, 0)
-
-    def arrived(pz):
+    lax.fori_loop(0, nz * SPLIT, place, 0)
+
+    def reduce_x(pz, s):
         for k in range(1, nx):
-            x_copy((x + k) % nx, pz, (x + k) % nx).wait_recv()
-
-    def reduced(pz, r):
-        value = part[x * share_x + pz * share_z + r]
-        for k in range(1, nx):
-            value = value + from_x[(x + k) % nx, pz, r]
-        return value
-
-    def z_copy(peer, slot):
-        return pltpu.make_async_remote_copy(
-            src_ref=z_out.at[peer],
-            dst_ref=from_z.at[slot],
-            send_sem=send6.at[peer],
-            recv_sem=recv6.at[slot],
+            x_copy((x + k) % nx, pz, s, (x + k) % nx).wait_recv()
+        for r in range(share):
+            value = part[row_of(x, pz, s) + r]
+            for k in range(1, nx):
+                value = value + from_x[(x + k) % nx, pz, s, r]
+            z_out[pz, s, r] = value
+
+    def z_copy(peer, s, slot):
+        return pltpu.make_async_remote_copy(
+            src_ref=z_out.at[peer, s],
+            dst_ref=from_z.at[slot, s],
+            send_sem=send6.at[peer, s],
+            recv_sem=recv6.at[slot, s],
             device_id={"views": in_z(peer)},
             device_id_type=MESH,
         )
 
+    def piece(px, pz, s):
+        return grad.at[pl.ds(row_of(px, pz, s), share)]
+
+    def give_x(step, px, pz, s, sem):
+        return pltpu.make_async_remote_copy(
+            src_ref=piece(px, pz, s),
+            dst_ref=piece(px, pz, s),
+            send_sem=send7.at[sem, pz, s],
+            recv_sem=recv7.at[px, pz, s],
+            device_id={"views": in_x((x + step) % nx)},
+            device_id_type=MESH,
+        )
+
+    def give_z(peer, px, pz, s):
+        return pltpu.make_async_remote_copy(
+            src_ref=piece(px, pz, s),
+            dst_ref=piece(px, pz, s),
+            send_sem=send8.at[peer, s],
+            recv_sem=recv7.at[px, pz, s],
+            device_id={"views": in_z(peer)},
+            device_id_type=MESH,
+        )
+
+    for s in range(SPLIT):
+        for k in range(1, nz):
+            reduce_x((zh + k) % nz, s)
+            z_copy((zh + k) % nz, s, zh).start()
+
+    steps = [1] if nx == 2 else [1, nx - 1]
+    sent, waited = [], set()
+
+    def give(copy):
+        copy.start()
+        sent.append(copy)
+
+    def spread_x(pz, s):
+        for sem, step in enumerate(steps):
+            give(give_x(step, x, pz, s, sem))
+
+    def receive(step, turn, s):
+        px, pz = (x + step) % nx, (zh + turn) % nz
+        give_x(0, px, pz, s, 0).wait_recv()
+        waited.add((step, turn, s))
+        return px, pz
+
+    def relay(turn, s):
+        if nx == 4:
+            onward = 1 if s % 2 == 0 else nx - 1
+            px, pz = receive(nx - onward, turn, s)
+            give(give_x(onward, px, pz, s, 2))
+
+    for s in range(SPLIT):
+        reduce_x(zh, s)
+        for k in range(1, nz):
+            z_copy((zh + k) % nz, s, (zh + k) % nz).wait_recv()
+        for r in range(share):
+            value = z_out[zh, s, r]
+            for k in range(1, nz):
+                value = value + from_z[(zh + k) % nz, s, r]
+            grad[row_of(x, zh, s) + r] = value
+        for k in range(1, nz):
+            give(give_z((zh + k) % nz, x, zh, s))
+        spread_x(zh, s)
+    for s in range(SPLIT):
+        relay(0, s)
+        for k in range(1, nz):
+            _, pz = receive(0, k, s)
+            spread_x(pz, s)
     for k in range(1, nz):
-        peer = (zh + k) % nz
-        arrived(peer)
-
-        def gather_z(r, carry):
-            z_out[peer, r] = reduced(peer, r)
-            return carry
-
-        lax.fori_loop(0, share_z, gather_z, 0)
-        z_copy(peer, zh).start()
-
-    arrived(zh)
-
-    def own(r, carry):
-        z_out[zh, r] = reduced(zh, r)
-        return carry
-
-    lax.fori_loop(0, share_z, own, 0)
-    for k in range(1, nz):
-        z_copy((zh + k) % nz, (zh + k) % nz).wait_recv()
-
-    def finish(r, carry):
-        value = z_out[zh, r]
-        for k in range(1, nz):
-            value = value + from_z[(zh + k) % nz, r]
-        grad[x * share_x + zh * share_z + r] = value
-        return carry
-
-    lax.fori_loop(0, share_z, finish, 0)
-
-    def piece(px, pz):
-        return grad.at[pl.ds(px * share_x + pz * share_z, share_z)]
-
-    def give_x(peer, px, pz):
-        return pltpu.make_async_remote_copy(
-            src_ref=piece(px, pz),
-            dst_ref=piece(px, pz),
-            send_sem=send7.at[peer, pz],
-            recv_sem=recv7.at[px, pz],
-            device_id={"views": in_x(peer)},
-            device_id_type=MESH,
-        )
-
-    def give_z(peer, px, pz):
-        return pltpu.make_async_remote_copy(
-            src_ref=piece(px, pz),
-            dst_ref=piece(px, pz),
-            send_sem=send8.at[peer],
-            recv_sem=recv7.at[px, pz],
-            device_id={"views": in_z(peer)},
-            device_id_type=MESH,
-        )
-
-    for k in range(1, nz):
-        give_z((zh + k) % nz, x, zh).start()
-    for k in range(1, nx):
-        give_x((x + k) % nx, x, zh).start()
-    for k in range(1, nz):
-        pz = (zh + k) % nz
-        give_z(pz, x, pz).wait_recv()
-        for m in range(1, nx):
-            give_x((x + m) % nx, x, pz).start()
+        for s in range(SPLIT):
+            relay(k, s)
     for k in range(nz):
-        pz = (zh + k) % nz
-        for m in range(1, nx):
-            give_x((x + m) % nx, (x + m) % nx, pz).wait_recv()
+        for s in range(SPLIT):
+            for step in range(1, nx):
+                if (step, k, s) not in waited:
+                    receive(step, k, s)
     for k in range(1, nc):
         total_copy((c + k) % nc, (c + k) % nc).wait_recv()
 
@@ -625,12 +669,13 @@
     for k in range(1, nx):
         peer = (x + k) % nx
         for pz in range(nz):
-            x_copy(peer, pz, x).wait_send()
-            give_x(peer, x, pz).wait_send()
+            for s in range(SPLIT):
+                x_copy(peer, pz, s, x).wait_send()
     for k in range(1, nz):
-        peer = (zh + k) % nz
-        z_copy(peer, zh).wait_send()
-        give_z(peer, x, zh).wait_send()
+        for s in range(SPLIT):
+            z_copy((zh + k) % nz, s, zh).wait_send()
+    for copy in sent:
+        copy.wait_send()
 
 
 def body(sizes, concentration, shear_index, shear_weight, attenuation, yields, line_energy, measured):
@@ -638,7 +683,9 @@
     views = shear_index.shape[0]
     nx, nz, ny, nc = sizes
     wide = views * width // nc
+    tiles = wide // LANES
     blocks = width // LANES
+    share = depth // nx // nz // SPLIT
     hbm = pl.BlockSpec(memory_space=pltpu.HBM)
     vmem = pl.BlockSpec(memory_space=pltpu.VMEM)
     full = depth * elements
@@ -653,7 +700,7 @@
         functools.partial(kernel, sizes),
         out_shape=(
             pltpu.VMEM((depth, elements, width), F32),
-            pltpu.VMEM((views, elements, width), F32),
+            pltpu.VMEM((views, elements, rows, width), F32),
         ),
         in_specs=[hbm] * 7,
         out_specs=(vmem, vmem),
@@ -673,28 +720,28 @@
         + [buf(views, depth, blocks + 5, elements, LANES)] * 2
         + [
             buf(PAIR, full, STEP),
-            buf(nc, 2 * elements, wide),
-            buf(nc, 2 * elements, wide),
+            buf(nc, tiles + tiles // 2, elements, LANES),
+            buf(nc, tiles + tiles // 2, elements, LANES),
             buf(nc, elements, wide),
             buf(nc, elements, wide),
-            buf(2 * elements, wide),
-            buf(ny, 2 * elements, wide),
+            buf(tiles + tiles // 2, elements, LANES),
+            buf(ny, tiles + tiles // 2, elements, LANES),
             buf(ny, elements, wide),
-            buf(nc, 2 * elements, wide),
-            buf(nc, 2 * elements, wide),
-            buf(elements, wide),
+            buf(nc, tiles + tiles // 2, elements, LANES),
+            buf(nc, tiles + tiles // 2, elements, LANES),
+            buf(elements, rows, wide),
             buf(depth, elements, width),
-            buf(nx, nz, depth // nx // nz, elements, width),
-            buf(nz, depth // nx // nz, elements, width),
-            buf(nz, depth // nx // nz, elements, width),
+            buf(nx, nz, SPLIT, share, elements, width),
+            buf(nz, SPLIT, share, elements, width),
+            buf(nz, SPLIT, share, elements, width),
         ]
         + [sems(nc)] * 2
         + [sems(ny)] * 2
         + [sems(nc)] * 4
-        + [sems(nx, nz)] * 2
-        + [sems(nz)] * 2
-        + [sems(nx, nz)] * 2
-        + [sems(nz)],
+        + [sems(nx, nz, SPLIT)] * 2
+        + [sems(nz, SPLIT)] * 2
+        + [sems(3, nz, SPLIT), sems(nx, nz, SPLIT)]
+        + [sems(nz, SPLIT)],
         compiler_params=pltpu.CompilerParams(
             collective_id=0, has_side_effects=True, vmem_limit_bytes=56 * 1024 * 1024
         ),
@@ -708,7 +755,7 @@
         measured,
     )
     gradient = jnp.transpose(gradient, (1, 0, 2)).reshape(elements, rows, depth, width)
-    return gradient, signal.reshape(views, elements, rows, width)
+    return gradient, signal
 
 
 SIZES = {(8, 64): (4, 2, 8, 8)}

time: 68.7 us -> 62.2 us (0.905)
  the two profiles are of different devices: /device:TPU:1 before, /device:TPU:12 now
where the time goes in v3:
time: 62.2 us; the launch traced here: 62.1 us
  Pallas kernels  59.2 us (95%)
  local copies, waits for them, and re-layouts  2.21 us (4%)
  between operations  0.64 us (1%)
    pallas_call x1, Pallas kernels, body(): pl.pallas_call(functools.partial(kernel, sizes), out_shape=(pltpu.VMEM((d...  59.2 us
    unnamed x2, local copies, waits for them, and re-layouts  2.21 us

profile of v3, /device:TPU:12, one launch (start us, length us, event | category | flops | bytes accessed | tf_op | source)
XLA Modules:
  0.0 62.1 jit_solution(3590063827253457337)
XLA Ops:
  0.6 59.2 %shard_map.86 = (f32[32,8,1024]{2,1,0:T(8,128)S(1)}, f32[2,8,1,1024]{3,2,1,0:T(1,128)S(1)}) custom-call(s32[2,32,1024]{2,1,0:T(8,128)} %index_in.1, f32[4,8]{1,0:T(4,128)} %att_in.1, f32[8]{0:T(128)} %yields_in.1, s32[8]{0:T(128)} %line_in.1, f32[8,32,1024]{2,1,0:T(8,128)} %bitcast.5, f32[2,32,1024]{2,1,0:T(8,128)} %weight_in.1, f32[2,8,1,1024]{3,2,1,0:T(1,128)} %measured_in.1), custom_call_target="tpu_custom_call" | custom-call | tf_op jit(solution)/shard_map/pallas_call | solution.py:699
  59.9 1.6 %copy.9 = f32[8,1,32,1024]{3,2,1,0:T(8,128)} copy(f32[8,1,32,1024]{3,0,2,1:T(8,128)S(1)} %bitcast.4) | data formatting | bytes 2097152
  61.5 0.6 %copy.11 = f32[2,8,1,1024]{3,2,1,0:T(1,128)} copy(f32[2,8,1,1024]{3,2,1,0:T(1,128)S(1)} %get-tuple-element.9) | data formatting | bytes 131072

commit v4 on v3

--- a/solution.py
+++ b/solution.py
@@ -75,6 +75,7 @@
     from_x,
     z_out,
     from_z,
+    full,
     send1,
     recv1,
     send2,
@@ -122,7 +123,7 @@
     own_at = pl.ds(own_base, wide)
     middle = width // 2
     fetches = [
-        pltpu.make_async_copy(src, dst, fetched.at[i])
+        pltpu.make_async_copy(src, dst, fetched.at[min(i, 6)])
         for i, (src, dst) in enumerate(
             [
                 (conc_in, conc),
@@ -140,6 +141,16 @@
 
     def start_of(v, d):
         return jnp.clip(shifts[v, d, 0] - (middle - LANES), 0, 2 * LANES)
+
+    def all_of(ref, sem):
+        return pltpu.make_async_remote_copy(
+            src_ref=ref,
+            dst_ref=ref,
+            send_sem=sem,
+            recv_sem=sem,
+            device_id={"depth": in_group(flip(1))},
+            device_id_type=MESH,
+        )
 
     barrier = pltpu.get_barrier_semaphore()
     greeted = 0
@@ -290,8 +301,8 @@
         return pltpu.make_async_remote_copy(
             src_ref=slab.at[k],
             dst_ref=group.at[c],
-            send_sem=send1.at[k],
-            recv_sem=recv1.at[c],
+            send_sem=send1.at[0],
+            recv_sem=recv1.at[0],
             device_id={"depth": in_group(k)},
             device_id_type=MESH,
         )
@@ -323,18 +334,7 @@
     lax.fori_loop(0, nc // PAIR, emit, 0)
     group[c] = slab[c]
 
-    def from_group(k):
-        return pltpu.make_async_remote_copy(
-            src_ref=slab.at[k],
-            dst_ref=group.at[k],
-            send_sem=send1.at[k],
-            recv_sem=recv1.at[k],
-            device_id={"depth": in_group(k)},
-            device_id_type=MESH,
-        )
-
-    for k in range(1, nc):
-        from_group((c + k) % nc).wait_recv()
+    all_of(group.at[: nc - 1], recv1.at[0]).wait_recv()
 
     line_wide = over(line_tile, wide)
 
@@ -376,8 +376,8 @@
         return pltpu.make_async_remote_copy(
             src_ref=group_send,
             dst_ref=group_recv.at[slot],
-            send_sem=send2.at[peer],
-            recv_sem=recv2.at[slot],
+            send_sem=send2.at[0],
+            recv_sem=recv2.at[0],
             device_id={"depth": in_y(peer)},
             device_id_type=MESH,
         )
@@ -385,8 +385,7 @@
     for k in sorted(range(1, ny), key=lambda k: -min(k, ny - k)):
         y_copy((y + k) % ny, y).start()
     group_recv[y] = group_send[...]
-    for k in range(1, ny):
-        y_copy((y + k) % ny, (y + k) % ny).wait_recv()
+    all_of(group_recv.at[: ny - 1], recv2.at[0]).wait_recv()
 
     total = jnp.zeros((TILE, wide), F32)
     prior = jnp.zeros((TILE, wide), F32)
@@ -397,8 +396,7 @@
         total += piece
         prior += jnp.where(j < y, piece, 0.0)
         following += jnp.where(j > y, piece, 0.0)
-    for fetch in fetches[6:]:
-        fetch.wait()
+    pltpu.make_async_copy(measured, measured, fetched.at[6]).wait()
     counts = total * (1.0 / depth_total)
     misfit = counts - jnp.concatenate([measured[e] for e in range(TILE)], axis=0)
     here_scale = group_scale[y]
@@ -427,7 +425,7 @@
         return pltpu.make_async_remote_copy(
             src_ref=back.at[peer],
             dst_ref=seeds.at[slot],
-            send_sem=send3.at[peer],
+            send_sem=send3.at[0],
             recv_sem=recv3.at[slot],
             device_id={"depth": in_group(peer)},
             device_id_type=MESH,
@@ -438,8 +436,8 @@
         return pltpu.make_async_remote_copy(
             src_ref=total_send,
             dst_ref=signal.at[slot // per_view, :, :, at],
-            send_sem=send4.at[peer],
-            recv_sem=recv4.at[slot],
+            send_sem=send4.at[0],
+            recv_sem=recv4.at[0],
             device_id={"depth": in_group(peer)},
             device_id_type=MESH,
         )
@@ -511,12 +509,13 @@
     def row_of(px, pz, s):
         return px * share_x + pz * share_z + s * share
 
-    def x_copy(peer, pz, s, slot):
+    def x_copy(k, pz, s):
+        peer = (x + k) % nx
         return pltpu.make_async_remote_copy(
             src_ref=part.at[pl.ds(row_of(peer, pz, s), share)],
-            dst_ref=from_x.at[slot, pz, s],
-            send_sem=send5.at[peer, pz, s],
-            recv_sem=recv5.at[slot, pz, s],
+            dst_ref=from_x.at[pz, s, k - 1],
+            send_sem=send5.at[0],
+            recv_sem=recv5.at[pz, s],
             device_id={"views": in_x(peer)},
             device_id_type=MESH,
         )
@@ -556,38 +555,37 @@
                 part[d, :, j * LANES : (j + 1) * LANES] = left + right
 
         for k in range(1, nx):
-            x_copy((x + k) % nx, pz, s, x).start()
+            x_copy(k, pz, s).start()
         return carry
 
     lax.fori_loop(0, nz * SPLIT, place, 0)
 
     def reduce_x(pz, s):
-        for k in range(1, nx):
-            x_copy((x + k) % nx, pz, s, (x + k) % nx).wait_recv()
+        all_of(from_x.at[pz, s], recv5.at[pz, s]).wait_recv()
         for r in range(share):
             value = part[row_of(x, pz, s) + r]
             for k in range(1, nx):
-                value = value + from_x[(x + k) % nx, pz, s, r]
+                value = value + from_x[pz, s, k - 1, r]
             z_out[pz, s, r] = value
 
     def z_copy(peer, s, slot):
         return pltpu.make_async_remote_copy(
             src_ref=z_out.at[peer, s],
             dst_ref=from_z.at[slot, s],
-            send_sem=send6.at[peer, s],
+            send_sem=send6.at[0],
             recv_sem=recv6.at[slot, s],
             device_id={"views": in_z(peer)},
             device_id_type=MESH,
         )
 
     def piece(px, pz, s):
-        return grad.at[pl.ds(row_of(px, pz, s), share)]
-
-    def give_x(step, px, pz, s, sem):
+        return full.at[pl.ds(row_of(px, pz, s), share)]
+
+    def give_x(step, px, pz, s):
         return pltpu.make_async_remote_copy(
             src_ref=piece(px, pz, s),
             dst_ref=piece(px, pz, s),
-            send_sem=send7.at[sem, pz, s],
+            send_sem=send7.at[0],
             recv_sem=recv7.at[px, pz, s],
             device_id={"views": in_x((x + step) % nx)},
             device_id_type=MESH,
@@ -597,7 +595,7 @@
         return pltpu.make_async_remote_copy(
             src_ref=piece(px, pz, s),
             dst_ref=piece(px, pz, s),
-            send_sem=send8.at[peer, s],
+            send_sem=send8.at[0],
             recv_sem=recv7.at[px, pz, s],
             device_id={"views": in_z(peer)},
             device_id_type=MESH,
@@ -609,19 +607,15 @@
             z_copy((zh + k) % nz, s, zh).start()
 
     steps = [1] if nx == 2 else [1, nx - 1]
-    sent, waited = [], set()
-
-    def give(copy):
-        copy.start()
-        sent.append(copy)
+    waited = set()
 
     def spread_x(pz, s):
-        for sem, step in enumerate(steps):
-            give(give_x(step, x, pz, s, sem))
+        for step in steps:
+            give_x(step, x, pz, s).start()
 
     def receive(step, turn, s):
         px, pz = (x + step) % nx, (zh + turn) % nz
-        give_x(0, px, pz, s, 0).wait_recv()
+        give_x(0, px, pz, s).wait_recv()
         waited.add((step, turn, s))
         return px, pz
 
@@ -629,7 +623,7 @@
         if nx == 4:
             onward = 1 if s % 2 == 0 else nx - 1
             px, pz = receive(nx - onward, turn, s)
-            give(give_x(onward, px, pz, s, 2))
+            give_x(onward, px, pz, s).start()
 
     for s in range(SPLIT):
         reduce_x(zh, s)
@@ -639,9 +633,9 @@
             value = z_out[zh, s, r]
             for k in range(1, nz):
                 value = value + from_z[(zh + k) % nz, s, r]
-            grad[row_of(x, zh, s) + r] = value
+            full[row_of(x, zh, s) + r] = value
         for k in range(1, nz):
-            give(give_z((zh + k) % nz, x, zh, s))
+            give_z((zh + k) % nz, x, zh, s).start()
         spread_x(zh, s)
     for s in range(SPLIT):
         relay(0, s)
@@ -651,31 +645,30 @@
     for k in range(1, nz):
         for s in range(SPLIT):
             relay(k, s)
-    for k in range(nz):
-        for s in range(SPLIT):
-            for step in range(1, nx):
+    def turn_out(px):
+        for o in range(share_x // TILE):
+            at = pl.ds(pl.multiple_of(px * share_x + o * TILE, TILE), TILE)
+            for j in range(blocks):
+                columns = slice(j * LANES, (j + 1) * LANES)
+                grad[:, at, columns] = jnp.transpose(full[at, :, columns], (1, 0, 2))
+
+    turn_out(x)
+    for step in [1, nx - 1, 2][: nx - 1]:
+        for k in range(nz):
+            for s in range(SPLIT):
                 if (step, k, s) not in waited:
                     receive(step, k, s)
-    for k in range(1, nc):
-        total_copy((c + k) % nc, (c + k) % nc).wait_recv()
-
-    for k in range(1, nc):
-        peer = (c + k) % nc
-        to_group(peer).wait_send()
-        seed_copy(peer, c).wait_send()
-        total_copy(peer, c).wait_send()
-    for k in range(1, ny):
-        y_copy((y + k) % ny, y).wait_send()
-    for k in range(1, nx):
-        peer = (x + k) % nx
-        for pz in range(nz):
-            for s in range(SPLIT):
-                x_copy(peer, pz, s, x).wait_send()
-    for k in range(1, nz):
-        for s in range(SPLIT):
-            z_copy((zh + k) % nz, s, zh).wait_send()
-    for copy in sent:
-        copy.wait_send()
+        turn_out((x + step) % nx)
+
+    all_of(signal.at[:, : nc - 1], recv4.at[0]).wait_recv()
+    all_of(slab.at[: nc - 1], send1.at[0]).wait_send()
+    all_of(group_recv.at[: ny - 1], send2.at[0]).wait_send()
+    all_of(back.at[: nc - 1], send3.at[0]).wait_send()
+    all_of(signal.at[:, : nc - 1], send4.at[0]).wait_send()
+    all_of(part.at[: (nx - 1) * share_x], send5.at[0]).wait_send()
+    all_of(z_out.at[: nz - 1], send6.at[0]).wait_send()
+    all_of(full.at[: (nx - 1) * share_x], send7.at[0]).wait_send()
+    all_of(z_out.at[: nz - 1], send8.at[0]).wait_send()
 
 
 def body(sizes, concentration, shear_index, shear_weight, attenuation, yields, line_energy, measured):
@@ -699,7 +692,7 @@
     gradient, signal = pl.pallas_call(
         functools.partial(kernel, sizes),
         out_shape=(
-            pltpu.VMEM((depth, elements, width), F32),
+            pltpu.VMEM((elements, depth, width), F32),
             pltpu.VMEM((views, elements, rows, width), F32),
         ),
         in_specs=[hbm] * 7,
@@ -712,7 +705,7 @@
             buf(elements, depth, width),
             buf(views, depth, width),
             buf(elements, rows, wide),
-            sems(6 + elements),
+            sems(7),
         ]
         + [pltpu.VMEM((full, full), BF16)] * 4
         + [buf(depth, blocks + 3, elements, LANES)] * 2
@@ -731,17 +724,16 @@
             buf(nc, tiles + tiles // 2, elements, LANES),
             buf(elements, rows, wide),
             buf(depth, elements, width),
-            buf(nx, nz, SPLIT, share, elements, width),
+            buf(nz, SPLIT, nx - 1, share, elements, width),
             buf(nz, SPLIT, share, elements, width),
             buf(nz, SPLIT, share, elements, width),
+            buf(depth, elements, width),
         ]
-        + [sems(nc)] * 2
-        + [sems(ny)] * 2
-        + [sems(nc)] * 4
-        + [sems(nx, nz, SPLIT)] * 2
-        + [sems(nz, SPLIT)] * 2
-        + [sems(3, nz, SPLIT), sems(nx, nz, SPLIT)]
-        + [sems(nz, SPLIT)],
+        + [sems(1)] * 5
+        + [sems(nc)]
+        + [sems(1)] * 3
+        + [sems(nz, SPLIT), sems(1), sems(nz, SPLIT)]
+        + [sems(1), sems(nx, nz, SPLIT), sems(1)],
         compiler_params=pltpu.CompilerParams(
             collective_id=0, has_side_effects=True, vmem_limit_bytes=56 * 1024 * 1024
         ),
@@ -754,8 +746,7 @@
         shear_weight,
         measured,
     )
-    gradient = jnp.transpose(gradient, (1, 0, 2)).reshape(elements, rows, depth, width)
-    return gradient, signal
+    return gradient.reshape(elements, rows, depth, width), signal
 
 
 SIZES = {(8, 64): (4, 2, 8, 8)}

time: 62.2 us -> 60.2 us (0.968)
  Pallas kernels: 59.2 us -> 57.8 us
    pallas_call x1, Pallas kernels: 59.2 us -> 57.8 us  [body(): pl.pallas_call(functools.partial(kernel, sizes), out_shape=(pltpu.VMEM((e...]
where the time goes in v4:
time: 60.2 us; the launch traced here: 60.1 us
  Pallas kernels  57.8 us (96%)
  local copies, waits for them, and re-layouts  1.6 us (3%)
  between operations  0.64 us (1%)
    pallas_call x1, Pallas kernels, body(): pl.pallas_call(functools.partial(kernel, sizes), out_shape=(pltpu.VMEM((e...  57.8 us
    unnamed x2, local copies, waits for them, and re-layouts  1.6 us

profile of v4, /device:TPU:12, one launch (start us, length us, event | category | flops | bytes accessed | tf_op | source)
XLA Modules:
  0.0 60.1 jit_solution(4311173738740085037)
XLA Ops:
  0.6 57.8 %shard_map.86 = (f32[8,32,1024]{2,1,0:T(8,128)S(1)}, f32[2,8,1,1024]{3,2,1,0:T(1,128)S(1)}) custom-call(s32[2,32,1024]{2,1,0:T(8,128)} %index_in.1, f32[4,8]{1,0:T(4,128)} %att_in.1, f32[8]{0:T(128)} %yields_in.1, s32[8]{0:T(128)} %line_in.1, f32[8,32,1024]{2,1,0:T(8,128)} %bitcast.5, f32[2,32,1024]{2,1,0:T(8,128)} %weight_in.1, f32[2,8,1,1024]{3,2,1,0:T(1,128)} %measured_in.1), custom_call_target="tpu_custom_call" | custom-call | tf_op jit(solution)/shard_map/pallas_call | solution.py:692
  58.5 1.0 %copy.12 = f32[8,1,32,1024]{3,2,1,0:T(8,128)} copy(f32[8,1,32,1024]{3,2,1,0:T(8,128)S(1)} %bitcast.4) | data formatting | bytes 2097152
  59.4 0.6 %copy.13 = f32[2,8,1,1024]{3,2,1,0:T(1,128)} copy(f32[2,8,1,1024]{3,2,1,0:T(1,128)S(1)} %get-tuple-element.9) | data formatting | bytes 131072

commit v5 on v4

--- a/solution.py
+++ b/solution.py
@@ -10,8 +10,8 @@
 LANES = 128
 TILE = 8
 STEP = 256
-PAIR = 2
-SPLIT = 4
+PAIR = 4
+HALVES = 1
 MESH = pl.DeviceIdType.MESH
 F32 = jnp.float32
 BF16 = jnp.bfloat16
@@ -91,6 +91,8 @@
     send7,
     recv7,
     send8,
+    recv8,
+    recv9,
 ):
     nx, nz, ny, nc = sizes
     views, depth, width = weight.shape
@@ -229,7 +231,7 @@
             part[at, :, columns] = jnp.transpose(conc[:, at, columns], (1, 0, 2))
         return carry
 
-    lax.fori_loop(0, depth // TILE, turn_rows, 0)
+    lax.fori_loop(0, depth // TILE, turn_rows, 0, unroll=True)
 
     def pad_row(d, carry):
         x_blocks = [part[d, :, j * LANES : (j + 1) * LANES] for j in range(blocks)]
@@ -256,7 +258,7 @@
             pad_step[d, j] = last - before_last
         return carry
 
-    lax.fori_loop(0, depth, pad_row, 0, unroll=4)
+    lax.fori_loop(0, depth, pad_row, 0, unroll=8)
 
     for fetch in fetches[1:3]:
         fetch.wait()
@@ -287,7 +289,7 @@
             return sums
 
         zero = jnp.zeros((TILE, LANES), F32)
-        sums = lax.fori_loop(0, depth // TILE, take_rows, (zero,) * blocks)
+        sums = lax.fori_loop(0, depth // TILE, take_rows, (zero,) * blocks, unroll=2)
         for j in range(0, blocks, 2):
             chunk, offset = divmod(v * blocks + j, tiles)
             levels = [
@@ -504,25 +506,29 @@
 
     share_x = depth // nx
     share_z = share_x // nz
-    share = share_z // SPLIT
-
-    def row_of(px, pz, s):
-        return px * share_x + pz * share_z + s * share
-
-    def x_copy(k, pz, s):
+    pieces = share_z * HALVES
+    half = width // HALVES
+
+    def row_of(px, pz, q):
+        return px * share_x + pz * share_z + q
+
+    def half_of(h):
+        return slice(h * half, (h + 1) * half)
+
+    def x_copy(k, pz, q, h):
         peer = (x + k) % nx
         return pltpu.make_async_remote_copy(
-            src_ref=part.at[pl.ds(row_of(peer, pz, s), share)],
-            dst_ref=from_x.at[pz, s, k - 1],
+            src_ref=part.at[row_of(peer, pz, q), :, half_of(h)],
+            dst_ref=from_x.at[pz, q, h, k - 1],
             send_sem=send5.at[0],
-            recv_sem=recv5.at[pz, s],
+            recv_sem=recv5.at[pz, q, h],
             device_id={"views": in_x(peer)},
             device_id_type=MESH,
         )
 
     def place(i, carry):
-        pz, s = (zh + 1 + i // SPLIT) % nz, i % SPLIT
-        for d in [row_of((x + 1 + k) % nx, pz, s) + r for k in range(nx) for r in range(share)]:
+        pz, q = (zh + 1 + i // share_z) % nz, i % share_z
+        for d in [row_of((x + 1 + k) % nx, pz, q) for k in range(nx)]:
             lefts = [None] * (blocks + 2)
             rights = [None] * (blocks + 2)
             for v in range(views):
@@ -554,19 +560,20 @@
                     left = left + jnp.where(lane == LANES - 2, high_left, 0.0)
                 part[d, :, j * LANES : (j + 1) * LANES] = left + right
 
+        for h in range(HALVES):
+            for k in range(1, nx):
+                x_copy(k, pz, q, h).start()
+        return carry
+
+    lax.fori_loop(0, nz * share_z, place, 0)
+
+    def reduce_x(pz, s):
+        q, h = divmod(s, HALVES)
+        all_of(from_x.at[pz, q, h], recv5.at[pz, q, h]).wait_recv()
+        value = part[row_of(x, pz, q), :, half_of(h)]
         for k in range(1, nx):
-            x_copy(k, pz, s).start()
-        return carry
-
-    lax.fori_loop(0, nz * SPLIT, place, 0)
-
-    def reduce_x(pz, s):
-        all_of(from_x.at[pz, s], recv5.at[pz, s]).wait_recv()
-        for r in range(share):
-            value = part[row_of(x, pz, s) + r]
-            for k in range(1, nx):
-                value = value + from_x[pz, s, k - 1, r]
-            z_out[pz, s, r] = value
+            value = value + from_x[pz, q, h, k - 1]
+        z_out[pz, s] = value
 
     def z_copy(peer, s, slot):
         return pltpu.make_async_remote_copy(
@@ -578,73 +585,63 @@
             device_id_type=MESH,
         )
 
-    def piece(px, pz, s):
-        return full.at[pl.ds(row_of(px, pz, s), share)]
-
-    def give_x(step, px, pz, s):
+    def give(to, px, pz, s, send, recv):
+        q, h = divmod(s, HALVES)
+        piece = full.at[row_of(px, pz, q), :, half_of(h)]
         return pltpu.make_async_remote_copy(
-            src_ref=piece(px, pz, s),
-            dst_ref=piece(px, pz, s),
-            send_sem=send7.at[0],
-            recv_sem=recv7.at[px, pz, s],
-            device_id={"views": in_x((x + step) % nx)},
+            src_ref=piece,
+            dst_ref=piece,
+            send_sem=send,
+            recv_sem=recv,
+            device_id={"views": to},
             device_id_type=MESH,
         )
 
     def give_z(peer, px, pz, s):
-        return pltpu.make_async_remote_copy(
-            src_ref=piece(px, pz, s),
-            dst_ref=piece(px, pz, s),
-            send_sem=send8.at[0],
-            recv_sem=recv7.at[px, pz, s],
-            device_id={"views": in_z(peer)},
-            device_id_type=MESH,
-        )
-
-    for s in range(SPLIT):
+        return give(in_z(peer), px, pz, s, send8.at[0], recv8.at[pz, s])
+
+    for s in range(pieces):
         for k in range(1, nz):
             reduce_x((zh + k) % nz, s)
             z_copy((zh + k) % nz, s, zh).start()
 
-    steps = [1] if nx == 2 else [1, nx - 1]
-    waited = set()
+    def onward(s):
+        return 1 if s % 2 == 0 else nx - 1
+
+    def to_relay(px, pz, s):
+        return give(in_x((px + onward(s)) % nx), px, pz, s, send7.at[0], recv7.at[pz, s])
 
     def spread_x(pz, s):
-        for step in steps:
-            give_x(step, x, pz, s).start()
-
-    def receive(step, turn, s):
-        px, pz = (x + step) % nx, (zh + turn) % nz
-        give_x(0, px, pz, s).wait_recv()
-        waited.add((step, turn, s))
-        return px, pz
+        to_relay(x, pz, s).start()
+        give(in_x((x + nx - onward(s)) % nx), x, pz, s, send7.at[0], recv9.at[0]).start()
 
     def relay(turn, s):
-        if nx == 4:
-            onward = 1 if s % 2 == 0 else nx - 1
-            px, pz = receive(nx - onward, turn, s)
-            give_x(onward, px, pz, s).start()
-
-    for s in range(SPLIT):
+        px, pz = (x + nx - onward(s)) % nx, (zh + turn) % nz
+        to_relay(px, pz, s).wait_recv()
+        give(in_x((x + onward(s)) % nx), px, pz, s, send7.at[0], recv9.at[1]).start()
+
+    for s in range(pieces):
         reduce_x(zh, s)
         for k in range(1, nz):
             z_copy((zh + k) % nz, s, (zh + k) % nz).wait_recv()
-        for r in range(share):
-            value = z_out[zh, s, r]
-            for k in range(1, nz):
-                value = value + from_z[(zh + k) % nz, s, r]
-            full[row_of(x, zh, s) + r] = value
+        value = z_out[zh, s]
+        for k in range(1, nz):
+            value = value + from_z[(zh + k) % nz, s]
+        q, h = divmod(s, HALVES)
+        full[row_of(x, zh, q), :, half_of(h)] = value
         for k in range(1, nz):
             give_z((zh + k) % nz, x, zh, s).start()
         spread_x(zh, s)
-    for s in range(SPLIT):
+    for s in range(pieces):
         relay(0, s)
         for k in range(1, nz):
-            _, pz = receive(0, k, s)
+            pz = (zh + k) % nz
+            give_z(pz, x, pz, s).wait_recv()
             spread_x(pz, s)
     for k in range(1, nz):
-        for s in range(SPLIT):
+        for s in range(pieces):
             relay(k, s)
+
     def turn_out(px):
         for o in range(share_x // TILE):
             at = pl.ds(pl.multiple_of(px * share_x + o * TILE, TILE), TILE)
@@ -653,12 +650,11 @@
                 grad[:, at, columns] = jnp.transpose(full[at, :, columns], (1, 0, 2))
 
     turn_out(x)
-    for step in [1, nx - 1, 2][: nx - 1]:
-        for k in range(nz):
-            for s in range(SPLIT):
-                if (step, k, s) not in waited:
-                    receive(step, k, s)
-        turn_out((x + step) % nx)
+    all_of(full.at[:share_x], recv9.at[0]).wait_recv()
+    turn_out((x + 1) % nx)
+    turn_out((x + nx - 1) % nx)
+    all_of(full.at[:share_x], recv9.at[1]).wait_recv()
+    turn_out((x + 2) % nx)
 
     all_of(signal.at[:, : nc - 1], recv4.at[0]).wait_recv()
     all_of(slab.at[: nc - 1], send1.at[0]).wait_send()
@@ -678,7 +674,7 @@
     wide = views * width // nc
     tiles = wide // LANES
     blocks = width // LANES
-    share = depth // nx // nz // SPLIT
+    share_z = depth // nx // nz
     hbm = pl.BlockSpec(memory_space=pltpu.HBM)
     vmem = pl.BlockSpec(memory_space=pltpu.VMEM)
     full = depth * elements
@@ -724,16 +720,16 @@
             buf(nc, tiles + tiles // 2, elements, LANES),
             buf(elements, rows, wide),
             buf(depth, elements, width),
-            buf(nz, SPLIT, nx - 1, share, elements, width),
-            buf(nz, SPLIT, share, elements, width),
-            buf(nz, SPLIT, share, elements, width),
+            buf(nz, share_z, HALVES, nx - 1, elements, width // HALVES),
+            buf(nz, share_z * HALVES, elements, width // HALVES),
+            buf(nz, share_z * HALVES, elements, width // HALVES),
             buf(depth, elements, width),
         ]
         + [sems(1)] * 5
         + [sems(nc)]
         + [sems(1)] * 3
-        + [sems(nz, SPLIT), sems(1), sems(nz, SPLIT)]
-        + [sems(1), sems(nx, nz, SPLIT), sems(1)],
+        + [sems(nz, share_z, HALVES), sems(1), sems(nz, share_z * HALVES)]
+        + [sems(1), sems(nz, share_z * HALVES), sems(1), sems(nz, share_z * HALVES), sems(2)],
         compiler_params=pltpu.CompilerParams(
             collective_id=0, has_side_effects=True, vmem_limit_bytes=56 * 1024 * 1024
         ),

time: 60.2 us -> 59.3 us (0.985)
  the two profiles are of different devices: /device:TPU:12 before, /device:TPU:4 now
where the time goes in v5:
time: 59.3 us; the launch traced here: 59.1 us
  Pallas kernels  56.9 us (96%)
  local copies, waits for them, and re-layouts  1.6 us (3%)
  between operations  0.64 us (1%)
    pallas_call x1, Pallas kernels, body(): pl.pallas_call(functools.partial(kernel, sizes), out_shape=(pltpu.VMEM((e...  56.9 us
    unnamed x2, local copies, waits for them, and re-layouts  1.6 us

profile of v5, /device:TPU:4, one launch (start us, length us, event | category | flops | bytes accessed | tf_op | source)
XLA Modules:
  0.0 59.1 jit_solution(15570743758312885954)
XLA Ops:
  0.6 56.9 %shard_map.86 = (f32[8,32,1024]{2,1,0:T(8,128)S(1)}, f32[2,8,1,1024]{3,2,1,0:T(1,128)S(1)}) custom-call(s32[2,32,1024]{2,1,0:T(8,128)} %index_in.1, f32[4,8]{1,0:T(4,128)} %att_in.1, f32[8]{0:T(128)} %yields_in.1, s32[8]{0:T(128)} %line_in.1, f32[8,32,1024]{2,1,0:T(8,128)} %bitcast.5, f32[2,32,1024]{2,1,0:T(8,128)} %weight_in.1, f32[2,8,1,1024]{3,2,1,0:T(1,128)} %measured_in.1), custom_call_target="tpu_custom_call" | custom-call | tf_op jit(solution)/shard_map/pallas_call | solution.py:688
  57.5 1.0 %copy.12 = f32[8,1,32,1024]{3,2,1,0:T(8,128)} copy(f32[8,1,32,1024]{3,2,1,0:T(8,128)S(1)} %bitcast.4) | data formatting | bytes 2097152
  58.5 0.6 %copy.13 = f32[2,8,1,1024]{3,2,1,0:T(1,128)} copy(f32[2,8,1,1024]{3,2,1,0:T(1,128)S(1)} %get-tuple-element.9) | data formatting | bytes 131072

commit v6 on v5

--- a/solution.py
+++ b/solution.py
@@ -450,8 +450,6 @@
     for e in range(TILE):
         total_send[e] = counts[e : e + 1]
         signal[own_view, e, :, own_at] = counts[e : e + 1]
-    for k in range(1, nc):
-        total_copy((c + k) % nc, c).start()
 
     def clear(d, carry):
         zeros = jnp.zeros((3, TILE, LANES), F32)
@@ -504,6 +502,8 @@
 
     lax.fori_loop(0, nc // PAIR, adjoint, 0)
 
+    for k in range(1, nc):
+        total_copy((c + k) % nc, c).start()
     share_x = depth // nx
     share_z = share_x // nz
     pieces = share_z * HALVES

time: 59.3 us -> 58.9 us (level)
  no operation moved by 1% of the time
where the time goes in v6:
time: 58.9 us; the launch traced here: 58.8 us
  Pallas kernels  56.5 us (96%)
  local copies, waits for them, and re-layouts  1.6 us (3%)
  between operations  0.64 us (1%)
    pallas_call x1, Pallas kernels, body(): pl.pallas_call(functools.partial(kernel, sizes), out_shape=(pltpu.VMEM((e...  56.5 us
    unnamed x2, local copies, waits for them, and re-layouts  1.6 us

profile of v6, /device:TPU:4, one launch (start us, length us, event | category | flops | bytes accessed | tf_op | source)
XLA Modules:
  0.0 58.8 jit_solution(11664071134494231688)
XLA Ops:
  0.6 56.5 %shard_map.86 = (f32[8,32,1024]{2,1,0:T(8,128)S(1)}, f32[2,8,1,1024]{3,2,1,0:T(1,128)S(1)}) custom-call(s32[2,32,1024]{2,1,0:T(8,128)} %index_in.1, f32[4,8]{1,0:T(4,128)} %att_in.1, f32[8]{0:T(128)} %yields_in.1, s32[8]{0:T(128)} %line_in.1, f32[8,32,1024]{2,1,0:T(8,128)} %bitcast.5, f32[2,32,1024]{2,1,0:T(8,128)} %weight_in.1, f32[2,8,1,1024]{3,2,1,0:T(1,128)} %measured_in.1), custom_call_target="tpu_custom_call" | custom-call | tf_op jit(solution)/shard_map/pallas_call | solution.py:688
  57.2 1.0 %copy.12 = f32[8,1,32,1024]{3,2,1,0:T(8,128)} copy(f32[8,1,32,1024]{3,2,1,0:T(8,128)S(1)} %bitcast.4) | data formatting | bytes 2097152
  58.1 0.6 %copy.13 = f32[2,8,1,1024]{3,2,1,0:T(1,128)} copy(f32[2,8,1,1024]{3,2,1,0:T(1,128)S(1)} %get-tuple-element.9) | data formatting | bytes 131072
